TPU v7x, 256 devices: a whole 4x4x8 slice. The times are simulated.
256 devices in a mesh: dp: 8 (over z), dap: 32 (over y, x, core).
Axes of the slice: x: 4, y: 4, z: 8, core: 2. Of those that a mesh axis runs over, the one named last changes fastest.
Arguments:
- pair_repr: bfloat16 [8, 256, 256, 128], P('dp', 'dap'), may hold values from -6 to 6
- lengths: int32 [8], P('dp'), may hold values from 128 to 256, as said below
- tri_project: bfloat16 [128, 512], P('dp'), may hold values from -0.5 to 0.5
- tri_gate: bfloat16 [128, 128], P('dp'), may hold values from -0.5 to 0.5
- tri_output: bfloat16 [128, 128], P('dp'), may hold values from -0.5 to 0.5
- attn_project: bfloat16 [128, 512], P('dp'), may hold values from -0.5 to 0.5
- attn_bias: bfloat16 [128, 4], P('dp'), may hold values from -60 to 60
- attn_output: bfloat16 [128, 128], P('dp'), may hold values from -0.5 to 0.5
- trans_expand: bfloat16 [128, 1024], P('dp'), may hold values from -0.5 to 0.5
- trans_reduce: bfloat16 [512, 128], P('dp'), may hold values from -0.25 to 0.25
Outputs:
- pair_out: bfloat16 [8, 256, 256, 128], P('dp', 'dap')
Inputs may be any that keep to these rules, and one draw needn't show every extreme that they name: `lengths`: at least one complex has exactly 256 tokens.
All inputs are finite; a program needn't handle non-finite values.
Results may differ from a plain program's by a relative error of at most 0.04.
Values may be sent and summed in bfloat16 or wider, within the bound.
A program may use at most 128 MiB of HBM per device.

v0:
```python
import jax
import jax.numpy as jnp
from jax import lax
from jax.sharding import PartitionSpec as P


def layer_norm(values):
    mean = jnp.mean(values, axis=-1, keepdims=True)
    centred = values - mean
    variance = jnp.mean(centred * centred, axis=-1, keepdims=True)
    return centred * lax.rsqrt(variance + 1e-05)


def matmul(left, right):
    shape = left.shape
    flat = left.reshape(-1, shape[-1])
    return jnp.dot(flat, right, preferred_element_type=jnp.float32).reshape(
        shape[:-1] + (right.shape[1],)
    )


def body(
    pair_repr,
    lengths,
    tri_project,
    tri_gate,
    tri_output,
    attn_project,
    attn_bias,
    attn_output,
    trans_expand,
    trans_reduce,
):
    gathered = (
        lax.all_gather(tri_project, "dp", axis=0, tiled=True),
        lax.all_gather(tri_gate, "dp", axis=0, tiled=True),
        lax.all_gather(tri_output, "dp", axis=0, tiled=True),
        lax.all_gather(attn_project, "dp", axis=0, tiled=True),
        lax.all_gather(attn_bias, "dp", axis=0, tiled=True),
        lax.all_gather(attn_output, "dp", axis=0, tiled=True),
        lax.all_gather(trans_expand, "dp", axis=0, tiled=True),
        lax.all_gather(trans_reduce, "dp", axis=0, tiled=True),
    )
    (
        tri_project,
        tri_gate,
        tri_output,
        attn_project,
        attn_bias,
        attn_output,
        trans_expand,
        trans_reduce,
    ) = gathered
    pair_in = pair_repr[0].astype(jnp.float32)
    row_count, token_count, channels = pair_in.shape
    head_count = attn_bias.shape[1]
    head_size = channels // head_count
    dap_index = lax.axis_index("dap")
    length = lengths[0]
    row_ids = dap_index * row_count + jnp.arange(row_count)
    valid_rows = (row_ids < length).astype(jnp.float32)
    valid_cols = (jnp.arange(token_count) < length).astype(jnp.float32)
    pair_mask = valid_rows[:, None] * valid_cols[None, :]
    normed = layer_norm(pair_in).astype(jnp.bfloat16)
    projected = matmul(normed, tri_project)
    left_proj = (
        jax.nn.sigmoid(projected[..., :channels])
        * projected[..., channels : 2 * channels]
        * pair_mask[..., None]
    ).astype(jnp.bfloat16)
    right_proj = (
        jax.nn.sigmoid(projected[..., 2 * channels : 3 * channels])
        * projected[..., 3 * channels :]
        * pair_mask[..., None]
    ).astype(jnp.bfloat16)
    gate_out = jax.nn.sigmoid(matmul(normed, tri_gate))
    contracted = jnp.einsum(
        "ikc,jkc->ijc",
        left_proj,
        lax.all_gather(right_proj, "dap", axis=0, tiled=True),
        preferred_element_type=jnp.float32,
    )
    contracted_norm = layer_norm(contracted).astype(jnp.bfloat16)
    first = pair_in + gate_out * matmul(contracted_norm, tri_output)
    first_norm = layer_norm(first).astype(jnp.bfloat16)
    bias_local = jnp.transpose(matmul(first_norm, attn_bias).astype(jnp.bfloat16), (2, 0, 1))
    bias_all = lax.all_gather(bias_local, "dap", axis=1, tiled=True)
    bias_ik = jnp.swapaxes(bias_all, 1, 2).astype(jnp.float32)
    attn_all = matmul(first_norm, attn_project)
    queries_rows = attn_all[..., :channels].astype(jnp.bfloat16)
    keys_rows = attn_all[..., channels : 2 * channels].astype(jnp.bfloat16)
    values_rows = attn_all[..., 2 * channels : 3 * channels].astype(jnp.bfloat16)
    gates_rows = attn_all[..., 3 * channels :].astype(jnp.bfloat16)
    queries, keys_all, values_all, gates = (
        lax.all_to_all(queries_rows, "dap", split_axis=1, concat_axis=0, tiled=True),
        lax.all_to_all(keys_rows, "dap", split_axis=1, concat_axis=0, tiled=True),
        lax.all_to_all(values_rows, "dap", split_axis=1, concat_axis=0, tiled=True),
        lax.all_to_all(gates_rows, "dap", split_axis=1, concat_axis=0, tiled=True),
    )
    col_count = queries.shape[1]
    queries = queries.reshape(token_count, col_count, head_count, head_size)
    keys_all = keys_all.reshape(token_count, col_count, head_count, head_size)
    values_all = values_all.reshape(token_count, col_count, head_count, head_size)
    inv_sqrt = 1.0 / head_size**0.5
    scores = (
        jnp.einsum("ijhd,kjhd->jhik", queries, keys_all, preferred_element_type=jnp.float32)
        * inv_sqrt
        + bias_ik[None]
    )
    scores = jnp.where(valid_cols[None, None, None, :] > 0, scores, -1000000000.0)
    soft = jax.nn.softmax(scores, axis=-1).astype(jnp.bfloat16)
    attended = jnp.einsum(
        "jhik,kjhd->ijhd", soft, values_all, preferred_element_type=jnp.float32
    ).reshape(token_count, col_count, channels)
    gated_out = (jax.nn.sigmoid(gates.astype(jnp.float32)) * attended).astype(jnp.bfloat16)
    gated_rows = lax.all_to_all(gated_out, "dap", split_axis=0, concat_axis=1, tiled=True)
    second = first + matmul(gated_rows, attn_output)
    second_norm = layer_norm(second).astype(jnp.bfloat16)
    expanded = matmul(second_norm, trans_expand)
    hidden_units = trans_reduce.shape[0]
    activated = (jax.nn.silu(expanded[..., :hidden_units]) * expanded[..., hidden_units:]).astype(
        jnp.bfloat16
    )
    pair_out = (second + matmul(activated, trans_reduce)).astype(jnp.bfloat16)
    return pair_out[None]


def solution(mesh):
    placed = (
        P("dp", "dap", None, None),
        P("dp"),
        P("dp", None),
        P("dp", None),
        P("dp", None),
        P("dp", None),
        P("dp", None),
        P("dp", None),
        P("dp", None),
        P("dp", None),
    )
    return jax.shard_map(
        body, mesh=mesh, in_specs=placed, out_specs=P("dp", "dap", None, None), check_vma=False
    )
```

profile of v0, /device:TPU:2, one launch (start us, length us, event | category | flops | bytes accessed | tf_op | source)
XLA Modules:
  0.0 366.0 jit_solution(8504436581596782671)
XLA Ops:
  6.5 1.2 copy.66
  8.1 28.5 %all_gather.31 = bf16[128,512]{1,0:T(8,128)(2,1)S(1)} all-gather(bf16[16,512]{1,0:T(8,128)(2,1)} %param.12), channel_id=1, replica_groups=mesh['dp'=8,'dap'=32] {'dp'}, dimensions={0}, use_global_device_ids=true | all-gather | bytes 147456 | tf_op jit(solution)/shard_map/all_gather | solution.py:35
  37.2 2.7 fusion.45
  40.0 2.8 fusion.35
  42.8 1.0 copy.71
  43.8 24.5 %all_gather.33 = bf16[128,128]{1,0:T(8,128)(2,1)S(1)} all-gather(bf16[16,128]{1,0:T(8,128)(2,1)S(1)} %copy-done.6), channel_id=1, replica_groups=mesh['dp'=8,'dap'=32] {'dp'}, dimensions={0}, use_global_device_ids=true | all-gather | bytes 36864 | tf_op jit(solution)/shard_map/all_gather | solution.py:37
  68.3 24.5 %all_gather.30 = bf16[128,128]{1,0:T(8,128)(2,1)S(1)} all-gather(bf16[16,128]{1,0:T(8,128)(2,1)S(1)} %copy-done.7), channel_id=1, replica_groups=mesh['dp'=8,'dap'=32] {'dp'}, dimensions={0}, use_global_device_ids=true | all-gather | bytes 36864 | tf_op jit(solution)/shard_map/all_gather | solution.py:36
  92.7 24.6 %all_gather.34 = bf16[128,512]{1,0:T(8,128)(2,1)S(1)} all-gather(bf16[16,512]{1,0:T(8,128)(2,1)S(1)} %copy-done.4), channel_id=1, replica_groups=mesh['dp'=8,'dap'=32] {'dp'}, dimensions={0}, use_global_device_ids=true | all-gather | bytes 147456 | tf_op jit(solution)/shard_map/all_gather | solution.py:38
  117.3 3.4 all-gather.3.cloned.1.call-done
  120.7 22.1 %copy.74 = bf16[256,256,128]{1,0,2:T(8,128)(2,1)} copy(bf16[256,256,128]{2,1,0:T(8,128)(2,1)} %all-gather.3.cloned.1.call-done) | data formatting | bytes 33554432 | tf_op jit(solution)/shard_map/all_gather | solution.py:80
  142.8 8.1 %fusion.71 = (f32[8,256]{1,0:T(8,128)S(1)}, f32[8,256,128]{1,0,2:T(8,128)S(1)}) fusion(bf16[256,256,128]{1,0,2:T(8,128)(2,1)} %copy.74, bf16[8,256,128]{1,2,0:T(8,128)(2,1)S(1)} %get-tuple-element.5), kind=kOutput, calls=%fused_computation.98 | convolution fusion | flops 134477824 | bytes 18358272 | tf_op jit(solution)/shard_map/ikc,jkc->ijc/dot_general | solution.py:77
  151.5 0.6 fusion.72
  152.2 0.7 convolution_convert_fusion
  153.0 0.4 fusion.70
  153.4 1.1 copy.85
  154.5 5.7 %all-to-all-start.2 = ((bf16[8,256,128]{2,0,1:T(8,128)(2,1)}), bf16[8,256,128]{2,0,1:T(8,128)(2,1)S(1)}, u32[]{:S(2)}, u32[]{:S(2)}) async-start(bf16[8,256,128]{2,0,1:T(8,128)(2,1)} %copy.85), calls=%async_computation.2 | async-start | bytes 1048576 | tf_op jit(solution)/shard_map/all_to_all | solution.py:95
  160.2 1.1 copy.88
  161.4 9.4 %all-to-all-done.2 = bf16[8,256,128]{2,0,1:T(8,128)(2,1)S(1)} async-done(((bf16[8,256,128]{2,0,1:T(8,128)(2,1)}), bf16[8,256,128]{2,0,1:T(8,128)(2,1)S(1)}, u32[]{:S(2)}, u32[]{:S(2)}) %all-to-all-start.2) | async-done | bytes 524320 | tf_op jit(solution)/shard_map/all_to_all | solution.py:95
  170.7 5.1 %all-to-all-start.3 = ((bf16[8,256,128]{2,0,1:T(8,128)(2,1)}), bf16[8,256,128]{2,0,1:T(8,128)(2,1)S(1)}, u32[]{:S(2)}, u32[]{:S(2)}) async-start(bf16[8,256,128]{2,0,1:T(8,128)(2,1)} %copy.88), calls=%async_computation.3 | async-start | bytes 1048576 | tf_op jit(solution)/shard_map/all_to_all | solution.py:96
  175.8 16.6 %all-gather = bf16[8,16,4]{1,2,0:T(4,128)(2,1)S(1)} all-gather(bf16[1,16,4]{1,2,0:T(4,128)(2,1)S(1)} %bitcast.98), channel_id=1, replica_groups=mesh['dp'=8,'dap'=32] {'dp'}, dimensions={0}, use_global_device_ids=true | all-gather | bytes 1152 | tf_op jit(solution)/shard_map/all_gather | solution.py:39
  192.5 1.2 copy.82
  193.7 7.5 %all-to-all-start.1 = ((bf16[8,256,128]{2,0,1:T(8,128)(2,1)}), bf16[8,256,128]{2,0,1:T(8,128)(2,1)}, u32[]{:S(2)}, u32[]{:S(2)}) async-start(bf16[8,256,128]{2,0,1:T(8,128)(2,1)} %copy.82), calls=%async_computation.1 | async-start | bytes 1048576 | tf_op jit(solution)/shard_map/all_to_all | solution.py:97
  201.4 25.7 %all_gather.36 = bf16[4,256,256]{2,0,1:T(4,128)(2,1)S(1)} all-gather(bf16[4,8,256]{2,0,1:T(4,128)(2,1)S(1)} %fusion.31), channel_id=1, replica_groups=mesh['dp'=8,'dap'=32] {'dap'}, dimensions={1}, use_global_device_ids=true | all-gather | bytes 540672 | tf_op jit(solution)/shard_map/all_gather | solution.py:87
  227.3 1.2 copy.95
  228.5 1.2 copy.78
  229.7 0.9 copy.87
  230.5 3.1 reshape.178
  233.6 1.9 copy.90
  235.6 4.0 %reshape.179 = bf16[256,8,4,32]{3,2,1,0:T(4,128)(2,1)} reshape(bf16[32,8,8,128]{3,2,1,0:T(8,128)(2,1)} %copy.90) | data formatting | bytes 1048576 | tf_op jit(solution)/shard_map/reshape | solution.py:102
  239.6 6.6 %all-to-all-start = ((bf16[8,256,128]{2,0,1:T(8,128)(2,1)}), bf16[8,256,128]{2,0,1:T(8,128)(2,1)}, u32[]{:S(2)}, u32[]{:S(2)}) async-start(bf16[8,256,128]{2,0,1:T(8,128)(2,1)} %copy.78), calls=%async_computation | async-start | bytes 1048576 | tf_op jit(solution)/shard_map/all_to_all | solution.py:98
  246.1 1.9 copy.84
  248.1 4.0 %reshape.177 = bf16[256,8,4,32]{3,2,1,0:T(4,128)(2,1)} reshape(bf16[32,8,8,128]{3,2,1,0:T(8,128)(2,1)} %copy.84) | data formatting | bytes 1048576 | tf_op jit(solution)/shard_map/reshape | solution.py:103
  252.0 3.3 fusion.9
  255.4 5.6 %fusion.73 = (f32[8,4,256]{2,1,0:T(4,128)S(1)}, f32[8,4,256,256]{2,3,1,0:T(8,128)}) fusion(f32[8,4,256,256]{2,3,1,0:T(8,128)S(1)} %fusion.9, f32[4,256,256]{1,2,0:T(8,128)S(1)} %copy-done.2, pred[256]{0:T(512)(128)(4,1)S(1)} %broadcast_compare_fusion), kind=kOutput, calls=%fused_computation.100 | output fusion | flops 16777472 | bytes 17858816 | tf_op jit(solution)/shard_map/sub | solution.py:111
  261.0 5.2 %fusion.7 = f32[8,4,32,256]{3,2,1,0:T(8,128)S(1)} fusion(f32[8,4,256,256]{2,3,1,0:T(8,128)} %get-tuple-element.16, f32[8,4,256]{2,1,0:T(4,128)S(1)} %get-tuple-element.15, bf16[256,8,4,32]{3,2,1,0:T(4,128)(2,1)S(1)} %copy-done), kind=kOutput, calls=%fused_computation.11 | convolution fusion | flops 138412032 | bytes 9994240 | tf_op jit(solution)/shard_map/jhik,kjhd->ijhd/dot_general | solution.py:112
  266.2 0.4 copy.98
  266.6 2.1 copy.79
  268.7 1.3 add_divide_fusion
  270.1 1.3 copy.80
  271.4 1.3 copy.81
  272.7 0.9 fusion.44
  273.6 7.4 %all-to-all-start.4 = ((bf16[256,8,128]{2,1,0:T(8,128)(2,1)}), bf16[256,8,128]{2,1,0:T(8,128)(2,1)S(1)}, u32[]{:S(2)}, u32[]{:S(2)}) async-start(bf16[256,8,128]{2,1,0:T(8,128)(2,1)} %fusion.44), calls=%async_computation.4 | async-start | bytes 1048576 | tf_op jit(solution)/shard_map/all_to_all | solution.py:116
  281.0 24.5 %all_gather.37 = bf16[128,128]{1,0:T(8,128)(2,1)S(1)} all-gather(bf16[16,128]{1,0:T(8,128)(2,1)S(1)} %copy-done.8), channel_id=1, replica_groups=mesh['dp'=8,'dap'=32] {'dp'}, dimensions={0}, use_global_device_ids=true | all-gather | bytes 36864 | tf_op jit(solution)/shard_map/all_gather | solution.py:40
  305.5 24.6 %all_gather.39 = bf16[512,128]{1,0:T(8,128)(2,1)S(1)} all-gather(bf16[64,128]{1,0:T(8,128)(2,1)S(1)} %copy-done.5), channel_id=1, replica_groups=mesh['dp'=8,'dap'=32] {'dp'}, dimensions={0}, use_global_device_ids=true | all-gather | bytes 147456 | tf_op jit(solution)/shard_map/all_gather | solution.py:42
  330.2 24.8 %all_gather.38 = bf16[128,1024]{1,0:T(8,128)(2,1)S(1)} all-gather(bf16[16,1024]{1,0:T(8,128)(2,1)S(1)} %copy-done.3), channel_id=1, replica_groups=mesh['dp'=8,'dap'=32] {'dp'}, dimensions={0}, use_global_device_ids=true | all-gather | bytes 294912 | tf_op jit(solution)/shard_map/all_gather | solution.py:41
  355.5 1.3 fusion.48
  356.7 1.4 fusion.28
  358.2 1.0 copy.102
  (50 shorter events, 2.1 us)
Async XLA Ops:
  6.5 114.1 %all-gather.3.cloned.1.call-start = ((), (), s32[]{:S(2)}) async-start(), calls=%async_computation.5 | async-start | bytes 17301504 | tf_op jit(solution)/shard_map/all_gather | solution.py:80
  39.9 3.9 %copy-start.6 = (bf16[16,128]{1,0:T(8,128)(2,1)S(1)}, bf16[16,128]{1,0:T(8,128)(2,1)}, u32[]{:S(2)}) copy-start(bf16[16,128]{1,0:T(8,128)(2,1)} %param.14) | copy-start | bytes 12292
  39.9 28.4 %copy-start.7 = (bf16[16,128]{1,0:T(8,128)(2,1)S(1)}, bf16[16,128]{1,0:T(8,128)(2,1)}, u32[]{:S(2)}) copy-start(bf16[16,128]{1,0:T(8,128)(2,1)} %param.13) | copy-start | bytes 12292
  39.9 52.8 %copy-start.4 = (bf16[16,512]{1,0:T(8,128)(2,1)S(1)}, bf16[16,512]{1,0:T(8,128)(2,1)}, u32[]{:S(2)}) copy-start(bf16[16,512]{1,0:T(8,128)(2,1)} %param.15) | copy-start | bytes 49156
  153.0 22.8 %copy-start.9 = (bf16[16,4]{0,1:T(4,128)(2,1)S(1)}, bf16[16,4]{0,1:T(4,128)(2,1)}, u32[]{:S(2)}) copy-start(bf16[16,4]{0,1:T(4,128)(2,1)} %param.16) | copy-start | bytes 388
  154.5 16.2 %all-to-all-start.2 = ((bf16[8,256,128]{2,0,1:T(8,128)(2,1)}), bf16[8,256,128]{2,0,1:T(8,128)(2,1)S(1)}, u32[]{:S(2)}, u32[]{:S(2)}) async-start(bf16[8,256,128]{2,0,1:T(8,128)(2,1)} %copy.85), calls=%async_computation.2 | async-start | bytes 1048576 | tf_op jit(solution)/shard_map/all_to_all | solution.py:95
  170.7 22.9 %all-to-all-start.3 = ((bf16[8,256,128]{2,0,1:T(8,128)(2,1)}), bf16[8,256,128]{2,0,1:T(8,128)(2,1)S(1)}, u32[]{:S(2)}, u32[]{:S(2)}) async-start(bf16[8,256,128]{2,0,1:T(8,128)(2,1)} %copy.88), calls=%async_computation.3 | async-start | bytes 1048576 | tf_op jit(solution)/shard_map/all_to_all | solution.py:96
  193.7 36.0 %copy-start.1 = (bf16[8,256,128]{2,0,1:T(8,128)(2,1)}, bf16[8,256,128]{2,0,1:T(8,128)(2,1)S(1)}, u32[]{:S(2)}) copy-start(bf16[8,256,128]{2,0,1:T(8,128)(2,1)S(1)} %all-to-all-done.3) | copy-start | bytes 1572868
  193.7 45.9 %all-to-all-start.1 = ((bf16[8,256,128]{2,0,1:T(8,128)(2,1)}), bf16[8,256,128]{2,0,1:T(8,128)(2,1)}, u32[]{:S(2)}, u32[]{:S(2)}) async-start(bf16[8,256,128]{2,0,1:T(8,128)(2,1)} %copy.82), calls=%async_computation.1 | async-start | bytes 1048576 | tf_op jit(solution)/shard_map/all_to_all | solution.py:97
  239.6 27.0 %all-to-all-start = ((bf16[8,256,128]{2,0,1:T(8,128)(2,1)}), bf16[8,256,128]{2,0,1:T(8,128)(2,1)}, u32[]{:S(2)}, u32[]{:S(2)}) async-start(bf16[8,256,128]{2,0,1:T(8,128)(2,1)} %copy.78), calls=%async_computation | async-start | bytes 1048576 | tf_op jit(solution)/shard_map/all_to_all | solution.py:98
  252.0 3.3 copy-start.2
  255.4 5.6 %copy-start = (bf16[256,8,4,32]{3,2,1,0:T(4,128)(2,1)S(1)}, bf16[256,8,4,32]{3,2,1,0:T(4,128)(2,1)}, u32[]{:S(2)}) copy-start(bf16[256,8,4,32]{3,2,1,0:T(4,128)(2,1)} %reshape.177) | copy-start | bytes 1572868
  270.0 11.0 %copy-start.8 = (bf16[16,128]{1,0:T(8,128)(2,1)S(1)}, bf16[16,128]{1,0:T(8,128)(2,1)}, u32[]{:S(2)}) copy-start(bf16[16,128]{1,0:T(8,128)(2,1)} %param.17) | copy-start | bytes 12292
  270.0 35.5 %copy-start.5 = (bf16[64,128]{1,0:T(8,128)(2,1)S(1)}, bf16[64,128]{1,0:T(8,128)(2,1)}, u32[]{:S(2)}) copy-start(bf16[64,128]{1,0:T(8,128)(2,1)} %param.19) | copy-start | bytes 49156
  270.1 60.1 %copy-start.3 = (bf16[16,1024]{1,0:T(8,128)(2,1)S(1)}, bf16[16,1024]{1,0:T(8,128)(2,1)}, u32[]{:S(2)}) copy-start(bf16[16,1024]{1,0:T(8,128)(2,1)} %param.18) | copy-start | bytes 98308
  273.6 81.3 %all-to-all-start.4 = ((bf16[256,8,128]{2,1,0:T(8,128)(2,1)}), bf16[256,8,128]{2,1,0:T(8,128)(2,1)S(1)}, u32[]{:S(2)}, u32[]{:S(2)}) async-start(bf16[256,8,128]{2,1,0:T(8,128)(2,1)} %fusion.44), calls=%async_computation.4 | async-start | bytes 1048576 | tf_op jit(solution)/shard_map/all_to_all | solution.py:116
Sparse Core Ops, SparseCore 0:
  43.9 76.7 all-gather.2
where the time goes:
time: 368 us; the launch traced here: 366 us
  blocking collectives  218 us (59%)
  local copies, waits for them, and re-layouts  52.7 us (14%)
  starting transfers between devices  32.2 us (9%)
  matrix products  24.1 us (7%)
  between operations  14.4 us (4%)
  waiting for transfers between devices  12.8 us (3%)
  other arithmetic  11.6 us (3%)
    all_gather x1, blocking collectives, body(): lax.all_gather(tri_project, 'dp', axis=0, tiled=True)  28.5 us
    all_gather x1, blocking collectives, body(): bias_all = lax.all_gather(bias_local, 'dap', axis=1, tiled=True)  25.7 us
    all_gather x1, blocking collectives, body(): lax.all_gather(trans_expand, 'dp', axis=0, tiled=True)  24.8 us
    all_gather x1, blocking collectives, body(): lax.all_gather(trans_reduce, 'dp', axis=0, tiled=True)  24.6 us
    all_gather x1, blocking collectives, body(): lax.all_gather(attn_project, 'dp', axis=0, tiled=True)  24.6 us
    all_gather x1, blocking collectives, body(): lax.all_gather(tri_output, 'dp', axis=0, tiled=True)  24.5 us
    all_gather x1, blocking collectives, body(): lax.all_gather(attn_output, 'dp', axis=0, tiled=True)  24.5 us
    all_gather x1, blocking collectives, body(): lax.all_gather(tri_gate, 'dp', axis=0, tiled=True)  24.5 us
  transfers between devices with their start and end apart: 6, of which 2 were waited for; matrix products, arithmetic and copies ran while one was open for 10% of the time, Pallas kernels for 0%

commit v1 on v0

v1 whole, which is shorter than its diff:
```python
import functools

import jax
import jax.numpy as jnp
from jax import lax
from jax.experimental import pallas as pl
from jax.experimental.pallas import tpu as pltpu
from jax.sharding import PartitionSpec as P

F32 = jnp.float32
BF16 = jnp.bfloat16
NN = (((1,), (0,)), ((), ()))
NT = (((1,), (1,)), ((), ()))
TN = (((0,), (0,)), ((), ()))
LOG2E = 1.4426950408889634
EPS = 1e-05

ROWS = 8
TOKENS = 256
C = 128
HEADS = 4
HEAD = 32
FF = 512
DAP = TOKENS // ROWS
HALF = C // 2


def dot(left, right, dims):
    return lax.dot_general(left, right, dims, preferred_element_type=F32)


def sigmoid(v):
    return 0.5 + 0.5 * jnp.tanh(0.5 * v)


def norm_over(values, axis):
    mean = jnp.mean(values, axis=axis, keepdims=True)
    centred = values - mean
    variance = jnp.mean(centred * centred, axis=axis, keepdims=True)
    return centred * lax.rsqrt(variance + EPS)


def transposed(value):
    return jnp.transpose(value.astype(F32)).astype(BF16)


def wait_bytes(ref, sem):
    pltpu.make_async_copy(ref, ref, sem).wait()


def body(
    dp_count,
    length_ref,
    x_ref,
    tri_project_ref,
    tri_gate_ref,
    tri_output_ref,
    attn_project_ref,
    attn_bias_ref,
    attn_output_ref,
    expand_ref,
    reduce_ref,
    out_ref,
    mix_stage,
    w_tri,
    w_mix,
    w_expand,
    w_reduce,
    wt_tri,
    wt_mix,
    wt_expand,
    wt_reduce,
    pair_stage,
    pair_recv,
    normed_rows,
    lr_rows,
    lr_stage,
    lr_recv,
    c_stage,
    c_recv,
    c_normed,
    x_cols,
    xt,
    gate_t,
    first_t,
    first_norm_t,
    bias_rows,
    bias_stage,
    bias_recv,
    bias_t,
    q_diag,
    k_cols,
    v_aug,
    og_t,
    gated,
    out_cols,
    out_stage,
    out_recv,
    out_rows,
    w_send,
    w_recv,
    pair_sems,
    lr_send,
    lr_recv_sem,
    c_send,
    c_recv_sem,
    bias_sems,
    out_send,
    out_recv_sem,
):
    me = lax.axis_index("dap")
    my_dp = lax.axis_index("dp")
    core = me % 2
    chip_x = (me // 2) % 4
    chip_y = me // 8
    length = length_ref[0]

    def peer(step):
        px = (chip_x + (step // 2) % 4) % 4
        py = (chip_y + step // 8) % 4
        return py * 8 + px * 2 + (core + step % 2) % 2

    def exchange(stage, recv, send_sem, recv_sem):
        def send(step, carry):
            target = peer(step)
            pltpu.make_async_remote_copy(
                src_ref=stage.at[target],
                dst_ref=recv.at[me],
                send_sem=send_sem,
                recv_sem=recv_sem,
                device_id={"dap": target},
                device_id_type=pl.DeviceIdType.MESH,
            ).start()
            return carry

        lax.fori_loop(1, DAP, send, 0)
        pltpu.make_async_copy(stage.at[me], recv.at[me], recv_sem).start()

    def weight_sends(source, dest, index):
        def send(step, carry):
            target = (my_dp + step) % dp_count
            pltpu.make_async_remote_copy(
                src_ref=source,
                dst_ref=dest.at[my_dp],
                send_sem=w_send.at[index],
                recv_sem=w_recv.at[index],
                device_id={"dp": target},
                device_id_type=pl.DeviceIdType.MESH,
            ).start()
            return carry

        lax.fori_loop(1, dp_count, send, 0)
        pltpu.make_async_copy(source, dest.at[my_dp], w_recv.at[index]).start()

    barrier = pltpu.get_barrier_semaphore()

    def greet(step, carry):
        pl.semaphore_signal(
            barrier, inc=1, device_id={"dap": peer(step)}, device_id_type=pl.DeviceIdType.MESH
        )
        return carry

    lax.fori_loop(1, DAP, greet, 0)

    def greet_dp(step, carry):
        pl.semaphore_signal(
            barrier,
            inc=1,
            device_id={"dp": (my_dp + step) % dp_count},
            device_id_type=pl.DeviceIdType.MESH,
        )
        return carry

    lax.fori_loop(1, dp_count, greet_dp, 0)

    def cut_pair(two, carry):
        start = pl.multiple_of(two * 16, 16)
        both = x_ref[0, :, pl.ds(start, 16), :].astype(F32)
        pair_stage[two * 2] = both[:, :8].reshape(64, C).astype(BF16)
        pair_stage[two * 2 + 1] = both[:, 8:].reshape(64, C).astype(BF16)
        return carry

    lax.fori_loop(0, DAP // 2, cut_pair, 0)
    mix_stage[:, 0:128] = tri_gate_ref[...]
    mix_stage[:, 128:256] = tri_output_ref[...]
    mix_stage[:, 256:768] = attn_project_ref[...]
    mix_stage[:, 768:896] = attn_output_ref[...]
    mix_stage[:, 896:1024] = jnp.zeros((mix_stage.shape[0], 128), BF16)
    mix_stage[:, 896:900] = attn_bias_ref[...]

    pl.semaphore_wait(barrier, DAP - 1 + dp_count - 1)

    weight_sends(tri_project_ref, w_tri, 0)
    exchange(pair_stage, pair_recv, pair_sems.at[0], pair_sems.at[1])
    weight_sends(mix_stage, w_mix, 1)
    weight_sends(expand_ref, w_expand, 2)
    weight_sends(reduce_ref, w_reduce, 3)

    def norm_row(row, carry):
        normed_rows[row] = norm_over(x_ref[0, row].astype(F32), 1).astype(BF16)
        return carry

    lax.fori_loop(0, ROWS, norm_row, 0)
    valid_cols = (lax.broadcasted_iota(jnp.int32, (1, TOKENS), 1) < length).astype(F32)

    wait_bytes(w_tri, w_recv.at[0])
    for part in range(4):
        wt_tri[part] = transposed(
            w_tri[:, :, part * C : (part + 1) * C].reshape(C, C)
        )

    for half in range(2):
        span = slice(half * HALF, (half + 1) * HALF)

        def project_row(row, carry):
            normed = normed_rows[row]
            valid_row = (me * ROWS + row < length).astype(F32)
            mask = valid_cols * valid_row
            for side in range(2):
                gate = dot(wt_tri[2 * side, span], normed, NT)
                value = dot(wt_tri[2 * side + 1, span], normed, NT)
                lr_rows_value = sigmoid(gate) * value * mask
                lr_rows[side, 0, pl.ds(row, HALF, stride=ROWS), :] = lr_rows_value[:, :128]
                lr_rows[side, 1, pl.ds(row, HALF, stride=ROWS), :] = lr_rows_value[:, 128:]
            return carry

        lax.fori_loop(0, ROWS, project_row, 0)
        for side in range(2):
            for lanes in range(2):
                lr_stage[half, :, side, :, lanes * 128 : (lanes + 1) * 128] = (
                    lr_rows[side, lanes].astype(BF16).reshape(DAP, 16, 128)
                )
        exchange(lr_stage.at[half], lr_recv.at[half], lr_send.at[half], lr_recv_sem.at[half])

    wait_bytes(w_mix, w_recv.at[1])
    for part in range(8):
        wt_mix[part] = transposed(w_mix[:, :, part * C : (part + 1) * C].reshape(C, C))
    wait_bytes(pair_recv, pair_sems.at[1])
    x_cols[...] = pair_recv[...].astype(F32).reshape(TOKENS * ROWS, C)

    def column_gate(col, carry):
        column = jnp.transpose(x_cols[pl.ds(col, TOKENS, stride=ROWS), :])
        xt[col] = column
        normed = norm_over(column, 0).astype(BF16)
        gate_t[col] = sigmoid(dot(wt_mix[0], normed, NN))
        return carry

    lax.fori_loop(0, ROWS, column_gate, 0)
    v_aug[...] = jnp.ones(v_aug.shape, BF16)
    q_diag[...] = jnp.zeros(q_diag.shape, BF16)

    for half in range(2):
        wait_bytes(lr_recv.at[half], lr_recv_sem.at[half])
        left = lr_recv[half, :, 0].astype(F32)
        right = lr_recv[half, :, 1].astype(F32)
        sums = []
        for channel in range(2):
            rows = slice(channel * ROWS, (channel + 1) * ROWS)
            left_c = left[:, rows].reshape(TOKENS, TOKENS).astype(BF16)
            right_c = right[:, rows].reshape(TOKENS, TOKENS).astype(BF16)
            sums.append(dot(right_c, left_c, NT).reshape(DAP, ROWS, TOKENS))
        c_stage[half] = jnp.concatenate(sums, axis=1).astype(BF16)
        exchange(c_stage.at[half], c_recv.at[half], c_send.at[half], c_recv_sem.at[half])
        if half == 0:
            wait_bytes(w_expand, w_recv.at[2])
            for part in range(8):
                wt_expand[part * C : (part + 1) * C] = transposed(
                    w_expand[:, :, part * C : (part + 1) * C].reshape(C, C)
                )
        else:
            wait_bytes(w_reduce, w_recv.at[3])
            w_reduce_all = w_reduce[...].reshape(FF, C)
            for part in range(FF // C):
                wt_reduce[:, part * C : (part + 1) * C] = transposed(
                    w_reduce_all[part * C : (part + 1) * C]
                )

    wait_bytes(c_recv.at[0], c_recv_sem.at[0])
    wait_bytes(c_recv.at[1], c_recv_sem.at[1])

    def c_sum(step, total):
        return total + c_recv[step // DAP, step % DAP].astype(F32)

    total = lax.fori_loop(0, HALF, c_sum, jnp.zeros((16, TOKENS), F32))
    mean = (total[:8] + total[8:]) * (1.0 / C)
    mean2 = jnp.concatenate([mean, mean], axis=0)

    def c_square(step, total):
        centred = c_recv[step // DAP, step % DAP].astype(F32) - mean2
        return total + centred * centred

    total = lax.fori_loop(0, HALF, c_square, jnp.zeros((16, TOKENS), F32))
    scale = lax.rsqrt((total[:8] + total[8:]) * (1.0 / C) + EPS)
    scale2 = jnp.concatenate([scale, scale], axis=0)

    def c_scale(step, carry):
        value = (c_recv[step // DAP, step % DAP].astype(F32) - mean2) * scale2
        start = pl.multiple_of(step * 16, 16)
        c_normed[0, pl.ds(start, 16), :] = value[:, :128]
        c_normed[1, pl.ds(start, 16), :] = value[:, 128:]
        return carry

    lax.fori_loop(0, HALF, c_scale, 0)

    def column_first(col, carry):
        normed = jnp.concatenate(
            [
                c_normed[0, pl.ds(col, C, stride=ROWS), :],
                c_normed[1, pl.ds(col, C, stride=ROWS), :],
            ],
            axis=1,
        ).astype(BF16)
        first = xt[col] + gate_t[col] * dot(wt_mix[1], normed, NN)
        first_t[col] = first
        first_norm = norm_over(first, 0).astype(BF16)
        first_norm_t[col] = first_norm
        bias = dot(wt_mix[7, 0:16], first_norm, NN)[:8]
        bias_rows[0, pl.ds(col, 8, stride=ROWS), :] = bias[:, :128]
        bias_rows[1, pl.ds(col, 8, stride=ROWS), :] = bias[:, 128:]
        return carry

    lax.fori_loop(0, ROWS, column_first, 0)
    for lanes in range(2):
        bias_stage[:, lanes * 128 : (lanes + 1) * 128] = bias_rows[lanes, 0 : HEADS * ROWS].astype(
            BF16
        )

    def send_bias(step, carry):
        pltpu.make_async_remote_copy(
            src_ref=bias_stage,
            dst_ref=bias_recv.at[me],
            send_sem=bias_sems.at[0],
            recv_sem=bias_sems.at[1],
            device_id={"dap": peer(step)},
            device_id_type=pl.DeviceIdType.MESH,
        ).start()
        return carry

    lax.fori_loop(1, DAP, send_bias, 0)
    pltpu.make_async_copy(bias_stage, bias_recv.at[me], bias_sems.at[1]).start()

    q_scale = LOG2E / HEAD**0.5

    def column_project(col, carry):
        first_norm = first_norm_t[col]
        query = (dot(wt_mix[2], first_norm, NN) * q_scale).astype(BF16)
        value = dot(wt_mix[4], first_norm, NN).astype(BF16)
        og_t[col] = sigmoid(dot(wt_mix[5], first_norm, NN))
        k_cols[col] = transposed(dot(wt_mix[3], first_norm, NN))
        for head in range(HEADS):
            rows = slice(head * HEAD, (head + 1) * HEAD)
            q_diag[col, head, rows, :] = query[rows]
            v_aug[col, head, 0:HEAD, :] = value[rows]
        return carry

    lax.fori_loop(0, ROWS, column_project, 0)

    wait_bytes(bias_recv, bias_sems.at[1])
    masked = jnp.where(
        lax.broadcasted_iota(jnp.int32, (TOKENS, TOKENS), 0) < length, 0.0, -1e9
    )
    for head in range(HEADS):
        rows = slice(head * ROWS, (head + 1) * ROWS)
        bias = bias_recv[:, (head // 2) * 16 : (head // 2) * 16 + 16].astype(F32)
        bias = bias[:, (head % 2) * ROWS : (head % 2 + 1) * ROWS].reshape(TOKENS, TOKENS)
        bias_t[head] = jnp.transpose(bias) * LOG2E + masked

    def column_attend(two, carry):
        for inner in range(2):
            col = two * 2 + inner
            keys = k_cols[col]
            for head in range(HEADS):
                rows = slice(head * HEAD, (head + 1) * HEAD)
                scores = dot(keys, q_diag[col, head], NN) + bias_t[head]
                top = jnp.max(scores, axis=0, keepdims=True)
                soft = jnp.exp2(scores - top).astype(BF16)
                summed = dot(v_aug[col, head], soft, NN)
                attended = summed[0:HEAD] * (1.0 / summed[HEAD : HEAD + 1])
                gated[rows, :] = (attended * og_t[col, rows, :]).astype(BF16)
            second = first_t[col] + dot(wt_mix[6], gated[...], NN)
            second_norm = norm_over(second, 0).astype(BF16)
            hidden = dot(wt_expand[0:FF], second_norm, NN)
            up = dot(wt_expand[FF : 2 * FF], second_norm, NN)
            activated = (hidden * sigmoid(hidden) * up).astype(BF16)
            result = second + dot(wt_reduce[...], activated, NN)
            out_cols[inner] = jnp.transpose(result)
        out_stage[two] = jnp.concatenate(
            [out_cols[0].reshape(DAP, ROWS, C), out_cols[1].reshape(DAP, ROWS, C)], axis=1
        ).astype(BF16)
        exchange(out_stage.at[two], out_recv.at[two], out_send.at[two], out_recv_sem.at[two])
        return carry

    lax.fori_loop(0, ROWS // 2, column_attend, 0)

    for two in range(ROWS // 2):
        wait_bytes(out_recv.at[two], out_recv_sem.at[two])
        out_rows[:, two * 16 : (two + 1) * 16] = out_recv[two].astype(F32)
    flat_rows = out_rows.reshape(TOKENS * ROWS, C)

    def store_row(row, carry):
        out_ref[0, row] = flat_rows[pl.ds(row, TOKENS, stride=ROWS), :].astype(BF16)
        return carry

    lax.fori_loop(0, ROWS, store_row, 0)

    others = pl.ds(0, DAP - 1)
    wait_bytes(w_tri.at[pl.ds(0, dp_count - 1)], w_send.at[0])
    wait_bytes(w_mix.at[pl.ds(0, dp_count - 1)], w_send.at[1])
    wait_bytes(w_expand.at[pl.ds(0, dp_count - 1)], w_send.at[2])
    wait_bytes(w_reduce.at[pl.ds(0, dp_count - 1)], w_send.at[3])
    wait_bytes(pair_stage.at[others], pair_sems.at[0])
    wait_bytes(bias_recv.at[others], bias_sems.at[0])
    for half in range(2):
        wait_bytes(lr_stage.at[half, others], lr_send.at[half])
        wait_bytes(c_stage.at[half, others], c_send.at[half])
    for two in range(ROWS // 2):
        wait_bytes(out_stage.at[two, others], out_send.at[two])


def fused(dp_count, pair_repr, lengths, *weights):
    slice_rows = C // dp_count
    vmem = pl.BlockSpec(memory_space=pltpu.VMEM)
    scratch = [
        pltpu.VMEM((slice_rows, 1024), BF16),
        pltpu.VMEM((dp_count, slice_rows, 512), BF16),
        pltpu.VMEM((dp_count, slice_rows, 1024), BF16),
        pltpu.VMEM((dp_count, slice_rows, 1024), BF16),
        pltpu.VMEM((dp_count, FF // dp_count, C), BF16),
        pltpu.VMEM((4, C, C), BF16),
        pltpu.VMEM((8, C, C), BF16),
        pltpu.VMEM((2 * FF, C), BF16),
        pltpu.VMEM((C, FF), BF16),
        pltpu.VMEM((DAP, 64, C), BF16),
        pltpu.VMEM((DAP, 64, C), BF16),
        pltpu.VMEM((ROWS, TOKENS, C), BF16),
        pltpu.VMEM((2, 2, HALF * ROWS, 128), F32),
        pltpu.VMEM((2, DAP, 2, 16, TOKENS), BF16),
        pltpu.VMEM((2, DAP, 2, 16, TOKENS), BF16),
        pltpu.VMEM((2, DAP, 16, TOKENS), BF16),
        pltpu.VMEM((2, DAP, 16, TOKENS), BF16),
        pltpu.VMEM((2, C * ROWS, 128), F32),
        pltpu.VMEM((TOKENS * ROWS, C), F32),
        pltpu.VMEM((ROWS, C, TOKENS), F32),
        pltpu.VMEM((ROWS, C, TOKENS), F32),
        pltpu.VMEM((ROWS, C, TOKENS), F32),
        pltpu.VMEM((ROWS, C, TOKENS), BF16),
        pltpu.VMEM((2, 64, 128), F32),
        pltpu.VMEM((HEADS * ROWS, TOKENS), BF16),
        pltpu.VMEM((DAP, HEADS * ROWS, TOKENS), BF16),
        pltpu.VMEM((HEADS, TOKENS, TOKENS), F32),
        pltpu.VMEM((ROWS, HEADS, C, TOKENS), BF16),
        pltpu.VMEM((ROWS, TOKENS, C), BF16),
        pltpu.VMEM((ROWS, HEADS, 48, TOKENS), BF16),
        pltpu.VMEM((ROWS, C, TOKENS), F32),
        pltpu.VMEM((C, TOKENS), BF16),
        pltpu.VMEM((2, TOKENS, C), F32),
        pltpu.VMEM((ROWS // 2, DAP, 16, C), BF16),
        pltpu.VMEM((ROWS // 2, DAP, 16, C), BF16),
        pltpu.VMEM((DAP, 64, C), F32),
        pltpu.SemaphoreType.DMA((4,)),
        pltpu.SemaphoreType.DMA((4,)),
        pltpu.SemaphoreType.DMA((2,)),
        pltpu.SemaphoreType.DMA((2,)),
        pltpu.SemaphoreType.DMA((2,)),
        pltpu.SemaphoreType.DMA((2,)),
        pltpu.SemaphoreType.DMA((2,)),
        pltpu.SemaphoreType.DMA((2,)),
        pltpu.SemaphoreType.DMA((ROWS // 2,)),
        pltpu.SemaphoreType.DMA((ROWS // 2,)),
    ]
    return pl.pallas_call(
        functools.partial(body, dp_count),
        out_shape=jax.ShapeDtypeStruct((1, ROWS, TOKENS, C), BF16),
        in_specs=[pl.BlockSpec(memory_space=pltpu.SMEM)] + [vmem] * 9,
        out_specs=vmem,
        scratch_shapes=scratch,
        compiler_params=pltpu.CompilerParams(
            collective_id=0, has_side_effects=True, vmem_limit_bytes=48 * 1024 * 1024
        ),
    )(lengths, pair_repr, *weights)


def solution(mesh):
    dp_count = mesh.shape["dp"]
    placed = (P("dp", "dap", None, None), P("dp")) + (P("dp", None),) * 8
    return jax.shard_map(
        functools.partial(fused, dp_count),
        mesh=mesh,
        in_specs=placed,
        out_specs=P("dp", "dap", None, None),
        check_vma=False,
    )
```

time: 368 us -> 85 us (0.23)
  the two profiles are of different devices: /device:TPU:2 before, /device:TPU:1 now
where the time goes in v1:
time: 85 us; the launch traced here: 84.5 us
  Pallas kernels  77.6 us (91%)
  local copies, waits for them, and re-layouts  6.22 us (7%)
    pallas_call x1, Pallas kernels, fused(): pl.pallas_call(functools.partial(body, dp_count), out_shape=jax.ShapeDtyp...  77.6 us
    unnamed x20, local copies, waits for them, and re-layouts  6.22 us

profile of v1, /device:TPU:1, one launch (start us, length us, event | category | flops | bytes accessed | tf_op | source)
XLA Modules:
  0.0 84.5 jit_solution(13399056847736302960)
XLA Ops:
  0.0 0.0 copy-start.8
  0.0 0.0 copy-start.5
  0.7 0.0 copy-done.8
  0.7 0.1 copy.11.attn_bias_ref
  0.8 0.0 copy-done.5
  0.8 0.0 copy-start
  0.8 1.0 %copy-done = bf16[1,8,256,128]{3,2,1,0:T(8,128)(2,1)S(1)} copy-done((bf16[1,8,256,128]{3,2,1,0:T(8,128)(2,1)S(1)}, bf16[1,8,256,128]{3,2,1,0:T(8,128)(2,1)}, u32[]{:S(2)}) %copy-start) | copy-done | bytes 524312
  1.8 0.0 copy-start.1
  1.8 0.8 copy-done.1
  2.6 0.0 copy-start.2
  2.6 0.7 copy-done.2
  3.3 0.0 copy-start.3
  3.3 0.7 copy-done.3
  4.0 0.0 copy-start.4
  4.0 0.7 copy-done.4
  4.8 0.0 copy-start.6
  4.8 0.7 copy-done.6
  5.4 0.0 copy-start.7
  5.4 0.7 copy-done.7
  6.1 77.6 %shard_map.100 = bf16[1,8,256,128]{3,2,1,0:T(8,128)(2,1)S(1)} custom-call(s32[1]{0:T(128)S(6)} %copy.13.length_ref, bf16[1,8,256,128]{3,2,1,0:T(8,128)(2,1)S(1)} %copy-done, bf16[16,512]{1,0:T(8,128)(2,1)S(1)} %copy-done.2, bf16[16,128]{1,0:T(8,128)(2,1)S(1)} %copy-done.5, bf16[16,128]{1,0:T(8,128)(2,1)S(1)} %copy-done.6, bf16[16,512]{1,0:T(8,128)(2,1)S(1)} %copy-done.3, ...), custom_call_target="tpu_custom_call" | custom-call | tf_op jit(solution)/shard_map/pallas_call | solution.py:471
  83.7 0.8 copy.14
Async XLA Ops:
  0.0 0.7 copy-start.8
  0.0 0.8 copy-start.5
  0.8 1.0 %copy-start = (bf16[1,8,256,128]{3,2,1,0:T(8,128)(2,1)S(1)}, bf16[1,8,256,128]{3,2,1,0:T(8,128)(2,1)}, u32[]{:S(2)}) copy-start(bf16[1,8,256,128]{3,2,1,0:T(8,128)(2,1)} %x_ref.1) | copy-start | bytes 1572868
  1.8 0.8 copy-start.1
  2.6 0.7 copy-start.2
  3.3 0.7 copy-start.3
  4.0 0.7 copy-start.4
  4.8 0.7 copy-start.6
  5.4 0.7 copy-start.7

commit v2 on v1

--- a/solution.py
+++ b/solution.py
@@ -21,8 +21,16 @@
 HEADS = 4
 HEAD = 32
 FF = 512
+VMEM_LIMIT = 64 * 1024 * 1024 - 65536
 DAP = TOKENS // ROWS
 HALF = C // 2
+
+
+OFFSETS = (
+    (2, 2), (2, 3), (3, 2), (2, 1), (1, 2), (0, 2), (2, 0), (3, 1),
+    (1, 3), (3, 3), (1, 1), (0, 3), (3, 0), (0, 1), (1, 0),
+)
+MESH = pl.DeviceIdType.MESH
 
 
 def dot(left, right, dims):
@@ -51,7 +59,7 @@
 def body(
     dp_count,
     length_ref,
-    x_ref,
+    x_hbm,
     tri_project_ref,
     tri_gate_ref,
     tri_output_ref,
@@ -61,6 +69,9 @@
     expand_ref,
     reduce_ref,
     out_ref,
+    x_ref,
+    bias_in,
+    bias_square,
     mix_stage,
     w_tri,
     w_mix,
@@ -78,7 +89,9 @@
     lr_recv,
     c_stage,
     c_recv,
-    c_normed,
+    c_values,
+    c_mean,
+    c_scale,
     x_cols,
     xt,
     gate_t,
@@ -107,33 +120,36 @@
     bias_sems,
     out_send,
     out_recv_sem,
+    load_sems,
+    ready_sem,
 ):
     me = lax.axis_index("dap")
     my_dp = lax.axis_index("dp")
     core = me % 2
     chip_x = (me // 2) % 4
     chip_y = me // 8
-    length = length_ref[0]
-
-    def peer(step):
-        px = (chip_x + (step // 2) % 4) % 4
-        py = (chip_y + step // 8) % 4
-        return py * 8 + px * 2 + (core + step % 2) % 2
+
+    sibling = me + 1 - 2 * core
+
+    def chip_of(off_x, off_y):
+        return (chip_y + off_y) % 4 * 4 + (chip_x + off_x) % 4
+
+    peers = []
+    for off_x, off_y in OFFSETS:
+        chip = chip_of(off_x, off_y)
+        peers += [chip * 2 + core, chip * 2 + 1 - core]
+    peers.append(sibling)
 
     def exchange(stage, recv, send_sem, recv_sem):
-        def send(step, carry):
-            target = peer(step)
+        for target in peers:
             pltpu.make_async_remote_copy(
                 src_ref=stage.at[target],
                 dst_ref=recv.at[me],
                 send_sem=send_sem,
                 recv_sem=recv_sem,
                 device_id={"dap": target},
-                device_id_type=pl.DeviceIdType.MESH,
+                device_id_type=MESH,
             ).start()
-            return carry
-
-        lax.fori_loop(1, DAP, send, 0)
         pltpu.make_async_copy(stage.at[me], recv.at[me], recv_sem).start()
 
     def weight_sends(source, dest, index):
@@ -145,33 +161,47 @@
                 send_sem=w_send.at[index],
                 recv_sem=w_recv.at[index],
                 device_id={"dp": target},
-                device_id_type=pl.DeviceIdType.MESH,
+                device_id_type=MESH,
             ).start()
             return carry
 
         lax.fori_loop(1, dp_count, send, 0)
         pltpu.make_async_copy(source, dest.at[my_dp], w_recv.at[index]).start()
 
+    load_x = pltpu.make_async_copy(x_hbm, x_ref, load_sems.at[0])
+    load_x.start()
+    loads = [
+        pltpu.make_async_copy(tri_gate_ref, mix_stage.at[:, 0:128], load_sems.at[1]),
+        pltpu.make_async_copy(tri_output_ref, mix_stage.at[:, 128:256], load_sems.at[2]),
+        pltpu.make_async_copy(attn_project_ref, mix_stage.at[:, 256:768], load_sems.at[3]),
+        pltpu.make_async_copy(attn_output_ref, mix_stage.at[:, 768:896], load_sems.at[4]),
+        pltpu.make_async_copy(attn_bias_ref, bias_in, load_sems.at[5]),
+    ]
+    for load in loads:
+        load.start()
+
     barrier = pltpu.get_barrier_semaphore()
 
-    def greet(step, carry):
-        pl.semaphore_signal(
-            barrier, inc=1, device_id={"dap": peer(step)}, device_id_type=pl.DeviceIdType.MESH
-        )
-        return carry
-
-    lax.fori_loop(1, DAP, greet, 0)
-
-    def greet_dp(step, carry):
+    for step in range(1, dp_count):
         pl.semaphore_signal(
             barrier,
             inc=1,
             device_id={"dp": (my_dp + step) % dp_count},
-            device_id_type=pl.DeviceIdType.MESH,
+            device_id_type=MESH,
         )
-        return carry
-
-    lax.fori_loop(1, dp_count, greet_dp, 0)
+    column_chips = [chip_of(0, off) * 2 + core for off in (2, 1, 3)]
+    row_group = []
+    for off in (2, 1, 3):
+        row_group += [chip_of(off, 0) * 2 + core, chip_of(off, 0) * 2 + 1 - core]
+    for target in column_chips + row_group + [sibling]:
+        pl.semaphore_signal(barrier, inc=1, device_id={"dap": target}, device_id_type=MESH)
+
+    pl.semaphore_wait(barrier, dp_count - 1 + 10)
+
+    for target in column_chips:
+        pl.semaphore_signal(ready_sem, inc=1, device_id={"dap": target}, device_id_type=MESH)
+    weight_sends(tri_project_ref, w_tri, 0)
+    load_x.wait()
 
     def cut_pair(two, carry):
         start = pl.multiple_of(two * 16, 16)
@@ -180,18 +210,15 @@
         pair_stage[two * 2 + 1] = both[:, 8:].reshape(64, C).astype(BF16)
         return carry
 
-    lax.fori_loop(0, DAP // 2, cut_pair, 0)
-    mix_stage[:, 0:128] = tri_gate_ref[...]
-    mix_stage[:, 128:256] = tri_output_ref[...]
-    mix_stage[:, 256:768] = attn_project_ref[...]
-    mix_stage[:, 768:896] = attn_output_ref[...]
-    mix_stage[:, 896:1024] = jnp.zeros((mix_stage.shape[0], 128), BF16)
-    mix_stage[:, 896:900] = attn_bias_ref[...]
-
-    pl.semaphore_wait(barrier, DAP - 1 + dp_count - 1)
-
-    weight_sends(tri_project_ref, w_tri, 0)
+    lax.fori_loop(0, DAP // 2, cut_pair, 0, unroll=2)
+    pl.semaphore_wait(ready_sem, 3)
     exchange(pair_stage, pair_recv, pair_sems.at[0], pair_sems.at[1])
+    for load in loads:
+        load.wait()
+    slice_rows = mix_stage.shape[0]
+    bias_square[...] = jnp.zeros((C, C), F32)
+    bias_square[0:HEADS, 0:slice_rows] = bias_in[...].astype(F32)
+    mix_stage[:, 896:1024] = jnp.transpose(bias_square[...])[0:slice_rows].astype(BF16)
     weight_sends(mix_stage, w_mix, 1)
     weight_sends(expand_ref, w_expand, 2)
     weight_sends(reduce_ref, w_reduce, 3)
@@ -200,7 +227,8 @@
         normed_rows[row] = norm_over(x_ref[0, row].astype(F32), 1).astype(BF16)
         return carry
 
-    lax.fori_loop(0, ROWS, norm_row, 0)
+    lax.fori_loop(0, ROWS, norm_row, 0, unroll=2)
+    length = length_ref[0]
     valid_cols = (lax.broadcasted_iota(jnp.int32, (1, TOKENS), 1) < length).astype(F32)
 
     wait_bytes(w_tri, w_recv.at[0])
@@ -224,7 +252,7 @@
                 lr_rows[side, 1, pl.ds(row, HALF, stride=ROWS), :] = lr_rows_value[:, 128:]
             return carry
 
-        lax.fori_loop(0, ROWS, project_row, 0)
+        lax.fori_loop(0, ROWS, project_row, 0, unroll=2)
         for side in range(2):
             for lanes in range(2):
                 lr_stage[half, :, side, :, lanes * 128 : (lanes + 1) * 128] = (
@@ -245,7 +273,7 @@
         gate_t[col] = sigmoid(dot(wt_mix[0], normed, NN))
         return carry
 
-    lax.fori_loop(0, ROWS, column_gate, 0)
+    lax.fori_loop(0, ROWS, column_gate, 0, unroll=2)
     v_aug[...] = jnp.ones(v_aug.shape, BF16)
     q_diag[...] = jnp.zeros(q_diag.shape, BF16)
 
@@ -275,41 +303,48 @@
                     w_reduce_all[part * C : (part + 1) * C]
                 )
 
-    wait_bytes(c_recv.at[0], c_recv_sem.at[0])
-    wait_bytes(c_recv.at[1], c_recv_sem.at[1])
-
-    def c_sum(step, total):
-        return total + c_recv[step // DAP, step % DAP].astype(F32)
-
-    total = lax.fori_loop(0, HALF, c_sum, jnp.zeros((16, TOKENS), F32))
-    mean = (total[:8] + total[8:]) * (1.0 / C)
-    mean2 = jnp.concatenate([mean, mean], axis=0)
-
-    def c_square(step, total):
-        centred = c_recv[step // DAP, step % DAP].astype(F32) - mean2
-        return total + centred * centred
-
-    total = lax.fori_loop(0, HALF, c_square, jnp.zeros((16, TOKENS), F32))
-    scale = lax.rsqrt((total[:8] + total[8:]) * (1.0 / C) + EPS)
-    scale2 = jnp.concatenate([scale, scale], axis=0)
-
-    def c_scale(step, carry):
-        value = (c_recv[step // DAP, step % DAP].astype(F32) - mean2) * scale2
-        start = pl.multiple_of(step * 16, 16)
-        c_normed[0, pl.ds(start, 16), :] = value[:, :128]
-        c_normed[1, pl.ds(start, 16), :] = value[:, 128:]
-        return carry
-
-    lax.fori_loop(0, HALF, c_scale, 0)
+    means = []
+    squares = []
+    for half in range(2):
+        wait_bytes(c_recv.at[half], c_recv_sem.at[half])
+
+        def c_sum(step, total):
+            for inner in range(4):
+                block = step * 4 + inner
+                value = c_recv[half, block].astype(F32)
+                start = pl.multiple_of(half * 512 + block * 16, 16)
+                c_values[0, pl.ds(start, 16), :] = value[:, :128]
+                c_values[1, pl.ds(start, 16), :] = value[:, 128:]
+                total = total + (value[:8] + value[8:])
+            return total
+
+        zero = jnp.zeros((ROWS, TOKENS), F32)
+        mean = lax.fori_loop(0, DAP // 4, c_sum, zero) * (1.0 / HALF)
+
+        def c_square(step, total):
+            for inner in range(4):
+                value = c_recv[half, step * 4 + inner].astype(F32)
+                first = value[:8] - mean
+                other = value[8:] - mean
+                total = total + (first * first + other * other)
+            return total
+
+        means.append(mean)
+        squares.append(lax.fori_loop(0, DAP // 4, c_square, zero))
+    apart = means[0] - means[1]
+    variance = (squares[0] + squares[1] + apart * apart * (0.5 * HALF)) * (1.0 / C)
+    c_mean[...] = (means[0] + means[1]) * 0.5
+    c_scale[...] = lax.rsqrt(variance + EPS)
 
     def column_first(col, carry):
-        normed = jnp.concatenate(
+        values = jnp.concatenate(
             [
-                c_normed[0, pl.ds(col, C, stride=ROWS), :],
-                c_normed[1, pl.ds(col, C, stride=ROWS), :],
+                c_values[0, pl.ds(col, C, stride=ROWS), :],
+                c_values[1, pl.ds(col, C, stride=ROWS), :],
             ],
             axis=1,
-        ).astype(BF16)
+        )
+        normed = ((values - c_mean[pl.ds(col, 1), :]) * c_scale[pl.ds(col, 1), :]).astype(BF16)
         first = xt[col] + gate_t[col] * dot(wt_mix[1], normed, NN)
         first_t[col] = first
         first_norm = norm_over(first, 0).astype(BF16)
@@ -319,24 +354,21 @@
         bias_rows[1, pl.ds(col, 8, stride=ROWS), :] = bias[:, 128:]
         return carry
 
-    lax.fori_loop(0, ROWS, column_first, 0)
+    lax.fori_loop(0, ROWS, column_first, 0, unroll=4)
     for lanes in range(2):
         bias_stage[:, lanes * 128 : (lanes + 1) * 128] = bias_rows[lanes, 0 : HEADS * ROWS].astype(
             BF16
         )
 
-    def send_bias(step, carry):
+    for target in peers:
         pltpu.make_async_remote_copy(
             src_ref=bias_stage,
             dst_ref=bias_recv.at[me],
             send_sem=bias_sems.at[0],
             recv_sem=bias_sems.at[1],
-            device_id={"dap": peer(step)},
-            device_id_type=pl.DeviceIdType.MESH,
+            device_id={"dap": target},
+            device_id_type=MESH,
         ).start()
-        return carry
-
-    lax.fori_loop(1, DAP, send_bias, 0)
     pltpu.make_async_copy(bias_stage, bias_recv.at[me], bias_sems.at[1]).start()
 
     q_scale = LOG2E / HEAD**0.5
@@ -353,7 +385,7 @@
             v_aug[col, head, 0:HEAD, :] = value[rows]
         return carry
 
-    lax.fori_loop(0, ROWS, column_project, 0)
+    lax.fori_loop(0, ROWS, column_project, 0, unroll=2)
 
     wait_bytes(bias_recv, bias_sems.at[1])
     masked = jnp.where(
@@ -401,7 +433,7 @@
         out_ref[0, row] = flat_rows[pl.ds(row, TOKENS, stride=ROWS), :].astype(BF16)
         return carry
 
-    lax.fori_loop(0, ROWS, store_row, 0)
+    lax.fori_loop(0, ROWS, store_row, 0, unroll=4)
 
     others = pl.ds(0, DAP - 1)
     wait_bytes(w_tri.at[pl.ds(0, dp_count - 1)], w_send.at[0])
@@ -420,7 +452,11 @@
 def fused(dp_count, pair_repr, lengths, *weights):
     slice_rows = C // dp_count
     vmem = pl.BlockSpec(memory_space=pltpu.VMEM)
+    anywhere = pl.BlockSpec(memory_space=pltpu.HBM)
     scratch = [
+        pltpu.VMEM((1, ROWS, TOKENS, C), BF16),
+        pltpu.VMEM((HEADS, slice_rows), BF16),
+        pltpu.VMEM((C, C), F32),
         pltpu.VMEM((slice_rows, 1024), BF16),
         pltpu.VMEM((dp_count, slice_rows, 512), BF16),
         pltpu.VMEM((dp_count, slice_rows, 1024), BF16),
@@ -439,6 +475,8 @@
         pltpu.VMEM((2, DAP, 16, TOKENS), BF16),
         pltpu.VMEM((2, DAP, 16, TOKENS), BF16),
         pltpu.VMEM((2, C * ROWS, 128), F32),
+        pltpu.VMEM((ROWS, TOKENS), F32),
+        pltpu.VMEM((ROWS, TOKENS), F32),
         pltpu.VMEM((TOKENS * ROWS, C), F32),
         pltpu.VMEM((ROWS, C, TOKENS), F32),
         pltpu.VMEM((ROWS, C, TOKENS), F32),
@@ -467,17 +505,19 @@
         pltpu.SemaphoreType.DMA((2,)),
         pltpu.SemaphoreType.DMA((ROWS // 2,)),
         pltpu.SemaphoreType.DMA((ROWS // 2,)),
+        pltpu.SemaphoreType.DMA((6,)),
+        pltpu.SemaphoreType.REGULAR,
     ]
     return pl.pallas_call(
         functools.partial(body, dp_count),
         out_shape=jax.ShapeDtypeStruct((1, ROWS, TOKENS, C), BF16),
-        in_specs=[pl.BlockSpec(memory_space=pltpu.SMEM)] + [vmem] * 9,
+        in_specs=[pl.BlockSpec(memory_space=pltpu.SMEM)] + [anywhere] * 9,
         out_specs=vmem,
         scratch_shapes=scratch,
         compiler_params=pltpu.CompilerParams(
-            collective_id=0, has_side_effects=True, vmem_limit_bytes=48 * 1024 * 1024
+            collective_id=0, has_side_effects=True, vmem_limit_bytes=VMEM_LIMIT
         ),
-    )(lengths, pair_repr, *weights)
+    )(lengths, pair_repr, *weights[:4], jnp.transpose(weights[4]), *weights[5:])
 
 
 def solution(mesh):

time: 85 us -> 70.7 us (0.83)
  Pallas kernels: 77.6 us -> 68 us
  local copies, waits for them, and re-layouts: 6.22 us -> 1.87 us
    pallas_call x1, Pallas kernels: 77.6 us -> 68 us  [fused(): pl.pallas_call(functools.partial(body, dp_count), out_shape=jax.ShapeDtyp...]
    unnamed x20 -> x1, local copies, waits for them, and re-layouts: 6.22 us -> 1.87 us
where the time goes in v2:
time: 70.7 us; the launch traced here: 70.6 us
  Pallas kernels  68 us (96%)
  local copies, waits for them, and re-layouts  1.87 us (3%)
    pallas_call x1, Pallas kernels, fused(): pl.pallas_call(functools.partial(body, dp_count), out_shape=jax.ShapeDtyp...  68 us
    unnamed x1, local copies, waits for them, and re-layouts  1.87 us

profile of v2, /device:TPU:1, one launch (start us, length us, event | category | flops | bytes accessed | tf_op | source)
XLA Modules:
  0.0 70.6 jit_solution(603780271581787616)
XLA Ops:
  0.7 68.0 %shard_map.100 = bf16[1,8,256,128]{3,2,1,0:T(8,128)(2,1)} custom-call(s32[1]{0:T(128)S(6)} %copy.12.length_ref, bf16[1,8,256,128]{3,2,1,0:T(8,128)(2,1)} %x_hbm.1, bf16[16,512]{1,0:T(8,128)(2,1)} %tri_project_ref.1, bf16[16,128]{1,0:T(8,128)(2,1)} %tri_gate_ref.1, bf16[16,128]{1,0:T(8,128)(2,1)} %tri_output_ref.1, bf16[16,512]{1,0:T(8,128)(2,1)} %attn_project_ref.1, ...), custom_call_target="tpu_custom_call" | custom-call | tf_op jit(solution)/shard_map/pallas_call | solution.py:511
  68.7 1.9 %copy.13 = bf16[1,8,256,128]{3,2,1,0:T(8,128)(2,1)} copy(bf16[1,8,256,128]{3,2,1,0:T(8,128)(2,1)} %shard_map.100) | data formatting | bytes 1048576

commit v3 on v2

v3 whole, which is shorter than its diff:
```python
import functools

import jax
import jax.numpy as jnp
from jax import lax
from jax.experimental import pallas as pl
from jax.experimental.pallas import tpu as pltpu
from jax.sharding import PartitionSpec as P

F32 = jnp.float32
BF16 = jnp.bfloat16
NN = (((1,), (0,)), ((), ()))
NT = (((1,), (1,)), ((), ()))
TN = (((0,), (0,)), ((), ()))
LOG2E = 1.4426950408889634
EPS = 1e-05

ROWS = 8
TOKENS = 256
C = 128
HEADS = 4
HEAD = 32
FF = 512
VMEM_LIMIT = 64 * 1024 * 1024 - 65536
DAP = TOKENS // ROWS
PARTS = 4
PART = C // PARTS
GROUP = ROWS // 2


OFFSETS = (
    (2, 2), (2, 3), (3, 2), (2, 1), (1, 2), (0, 2), (2, 0), (3, 1),
    (1, 3), (3, 3), (1, 1), (0, 3), (3, 0), (0, 1), (1, 0),
)
MESH = pl.DeviceIdType.MESH


def dot(left, right, dims):
    return lax.dot_general(left, right, dims, preferred_element_type=F32)


def sigmoid(v):
    return 0.5 + 0.5 * jnp.tanh(0.5 * v)


def norm_over(values, axis):
    mean = jnp.mean(values, axis=axis, keepdims=True)
    centred = values - mean
    variance = jnp.mean(centred * centred, axis=axis, keepdims=True)
    return centred * lax.rsqrt(variance + EPS)


def transposed(value):
    return jnp.transpose(value.astype(F32)).astype(BF16)


def wait_bytes(ref, sem):
    pltpu.make_async_copy(ref, ref, sem).wait()


def body(
    dp_count,
    length_ref,
    x_hbm,
    tri_project_ref,
    tri_gate_ref,
    tri_output_ref,
    attn_project_ref,
    attn_bias_ref,
    attn_output_ref,
    expand_ref,
    reduce_ref,
    out_ref,
    x_ref,
    bias_in,
    bias_square,
    tri_in,
    tri_stage,
    mix_stage,
    w_tri,
    w_mix,
    w_expand,
    w_reduce,
    wt_tri,
    wt_mix,
    wt_expand,
    wt_reduce,
    pair_stage,
    pair_recv,
    normed_rows,
    lr_rows,
    lr_stage,
    lr_recv,
    c_stage,
    c_recv,
    c_values,
    c_mean,
    c_scale,
    x_cols,
    xt,
    gate_t,
    first_t,
    first_norm_t,
    bias_rows,
    bias_stage,
    bias_recv,
    bias_t,
    q_diag,
    k_cols,
    v_aug,
    og_t,
    scores_ref,
    out_stage,
    out_recv,
    out_rows,
    w_send,
    w_recv,
    relay_send,
    relay_recv,
    pair_sems,
    lr_send,
    lr_recv_sem,
    c_send,
    c_recv_sem,
    bias_send,
    bias_recv_sem,
    bias_relay_send,
    bias_relay_recv,
    out_send,
    out_recv_sem,
    load_sems,
    ready_sem,
):
    me = lax.axis_index("dap")
    my_dp = lax.axis_index("dp")
    core = me % 2
    my_chip = me // 2
    chip_x = (me // 2) % 4
    chip_y = me // 8

    sibling = me + 1 - 2 * core

    def chip_of(off_x, off_y):
        return (chip_y + off_y) % 4 * 4 + (chip_x + off_x) % 4

    peers = []
    same_core = []
    unheard = []
    for off_x, off_y in OFFSETS:
        chip = chip_of(off_x, off_y)
        both = [chip * 2 + core, chip * 2 + 1 - core]
        peers += both
        same_core += both[:1]
        if off_y != 0:
            unheard += both if off_x != 0 else both[1:]
    peers.append(sibling)

    def send_blocks(targets, stage, recv, send_sem, recv_sem):
        for target in targets:
            pltpu.make_async_remote_copy(
                src_ref=stage.at[target],
                dst_ref=recv.at[me],
                send_sem=send_sem,
                recv_sem=recv_sem,
                device_id={"dap": target},
                device_id_type=MESH,
            ).start()

    pending = []

    def exchange(stage, recv, send_sem, recv_sem):
        send_blocks(peers, stage, recv, send_sem, recv_sem)
        pltpu.make_async_copy(stage.at[me], recv.at[me], recv_sem).start()
        pending.append((stage.at[pl.ds(0, DAP - 1)], send_sem))

    def weight_sends(source, dest, index):
        def send(step, carry):
            target = (my_dp + step) % dp_count
            pltpu.make_async_remote_copy(
                src_ref=source,
                dst_ref=dest.at[my_dp],
                send_sem=w_send.at[index],
                recv_sem=w_recv.at[index],
                device_id={"dp": target},
                device_id_type=MESH,
            ).start()
            return carry

        lax.fori_loop(1, dp_count, send, 0)
        pltpu.make_async_copy(source, dest.at[my_dp], w_recv.at[index]).start()
        pending.append((dest.at[pl.ds(0, dp_count - 1)], w_send.at[index]))

    load_x = pltpu.make_async_copy(x_hbm, x_ref, load_sems.at[0])
    load_x.start()
    load_tri = pltpu.make_async_copy(tri_project_ref, tri_in, load_sems.at[7])
    load_tri.start()
    loads = [
        pltpu.make_async_copy(tri_gate_ref, mix_stage.at[0, :, 0:128], load_sems.at[1]),
        pltpu.make_async_copy(tri_output_ref, mix_stage.at[0, :, 128:256], load_sems.at[2]),
        pltpu.make_async_copy(
            attn_project_ref.at[:, 0:256], mix_stage.at[0, :, 256:512], load_sems.at[3]
        ),
        pltpu.make_async_copy(
            attn_project_ref.at[:, 256:512], mix_stage.at[1, :, 0:256], load_sems.at[6]
        ),
        pltpu.make_async_copy(attn_output_ref, mix_stage.at[1, :, 256:384], load_sems.at[4]),
        pltpu.make_async_copy(attn_bias_ref, bias_in, load_sems.at[5]),
    ]
    for load in loads:
        load.start()

    def relay(weights, index):
        wait_bytes(weights.at[0], w_recv.at[index])
        pltpu.make_async_remote_copy(
            src_ref=weights.at[core],
            dst_ref=weights.at[core],
            send_sem=relay_send.at[index],
            recv_sem=relay_recv.at[index],
            device_id={"dap": sibling},
            device_id_type=MESH,
        ).start()
        pending.append((weights.at[0], relay_send.at[index]))

    barrier = pltpu.get_barrier_semaphore()

    for step in range(1, dp_count):
        pl.semaphore_signal(
            barrier,
            inc=1,
            device_id={"dp": (my_dp + step) % dp_count},
            device_id_type=MESH,
        )
    column_chips = [chip_of(0, off) * 2 + core for off in (2, 1, 3)]
    row_group = []
    for off in (2, 1, 3):
        row_group += [chip_of(off, 0) * 2 + core, chip_of(off, 0) * 2 + 1 - core]
    for target in column_chips + row_group + [sibling]:
        pl.semaphore_signal(barrier, inc=1, device_id={"dap": target}, device_id_type=MESH)

    load_tri.wait()
    tri_whole = tri_in[...].astype(F32)
    for quarter in range(PARTS):
        tri_stage[quarter] = jnp.concatenate(
            [
                tri_whole[:, part * C + quarter * PART : part * C + (quarter + 1) * PART]
                for part in range(4)
            ],
            axis=1,
        ).astype(BF16)

    load_x.wait()

    def cut_pair(two, carry):
        start = pl.multiple_of(two * 16, 16)
        both = x_ref[0, :, pl.ds(start, 16), :].astype(F32)
        pair_stage[two * 2] = both[:, :8].reshape(64, C).astype(BF16)
        pair_stage[two * 2 + 1] = both[:, 8:].reshape(64, C).astype(BF16)
        return carry

    lax.fori_loop(0, DAP // 2, cut_pair, 0, unroll=2)

    def norm_row(row, carry):
        normed_rows[row] = norm_over(x_ref[0, row].astype(F32), 1).astype(BF16)
        return carry

    lax.fori_loop(0, ROWS, norm_row, 0, unroll=2)
    pl.semaphore_wait(barrier, dp_count - 1 + 10)

    for target in column_chips:
        pl.semaphore_signal(ready_sem, inc=1, device_id={"dap": target}, device_id_type=MESH)
    weight_sends(tri_stage.at[0], w_tri.at[0], 4)
    heard = row_group + column_chips + [sibling]
    send_blocks(heard, pair_stage, pair_recv, pair_sems.at[0], pair_sems.at[1])

    for quarter in range(1, PARTS):
        weight_sends(tri_stage.at[quarter], w_tri.at[quarter], 4 + quarter)
    pl.semaphore_wait(ready_sem, 3)
    send_blocks(unheard, pair_stage, pair_recv, pair_sems.at[0], pair_sems.at[1])
    pltpu.make_async_copy(pair_stage.at[me], pair_recv.at[me], pair_sems.at[1]).start()
    pending.append((pair_stage.at[pl.ds(0, DAP - 1)], pair_sems.at[0]))

    length = length_ref[0]
    valid_cols = (lax.broadcasted_iota(jnp.int32, (1, TOKENS), 1) < length).astype(F32)

    for quarter in range(PARTS):
        wait_bytes(w_tri.at[quarter], w_recv.at[4 + quarter])
        wt_tri[quarter] = transposed(w_tri[quarter].reshape(C, C))

        def project_row(row, carry):
            valid_row = (me * ROWS + row < length).astype(F32)
            mask = valid_cols * valid_row
            projected = dot(wt_tri[quarter], normed_rows[row], NT)
            for side in range(2):
                gate = projected[2 * side * PART : (2 * side + 1) * PART]
                value = projected[(2 * side + 1) * PART : (2 * side + 2) * PART]
                kept = sigmoid(gate) * value * mask
                lr_rows[side, 0, pl.ds(row, PART, stride=ROWS), :] = kept[:, :128]
                lr_rows[side, 1, pl.ds(row, PART, stride=ROWS), :] = kept[:, 128:]
            return carry

        lax.fori_loop(0, ROWS, project_row, 0, unroll=4)
        for lanes in range(2):
            lr_stage[quarter, :, :, lanes * 128 : (lanes + 1) * 128] = jnp.concatenate(
                [lr_rows[side, lanes].reshape(DAP, ROWS, 128) for side in range(2)], axis=1
            ).astype(BF16)
        exchange(
            lr_stage.at[quarter],
            lr_recv.at[quarter],
            lr_send.at[quarter],
            lr_recv_sem.at[quarter],
        )
        if quarter > 0:
            continue

        for load in loads:
            load.wait()
        slice_rows = mix_stage.shape[1]
        bias_square[...] = jnp.zeros((C, C), F32)
        bias_square[0:HEADS, 0:slice_rows] = bias_in[...].astype(F32)
        mix_stage[1, :, 384:512] = jnp.transpose(bias_square[...])[0:slice_rows].astype(BF16)
        lanes = pl.ds(pl.multiple_of(core * FF, FF), FF)
        rows_sent = reduce_ref.shape[0] // 2
        rows = pl.ds(pl.multiple_of(core * rows_sent, rows_sent), rows_sent)
        weight_sends(mix_stage.at[core], w_mix.at[core], 1)
        weight_sends(expand_ref.at[:, lanes], w_expand.at[core], 2)
        weight_sends(reduce_ref.at[rows, :], w_reduce.at[core], 3)

    relay(w_mix, 1)
    wait_bytes(pair_recv, pair_sems.at[1])
    x_cols[...] = pair_recv[...].astype(F32).reshape(TOKENS * ROWS, C)

    wait_bytes(w_mix.at[0], relay_recv.at[1])
    for part in range(8):
        wt_mix[part] = transposed(
            w_mix[part // 4, :, :, (part % 4) * C : (part % 4 + 1) * C].reshape(C, C)
        )

    def column_gate(col, carry):
        column = jnp.transpose(x_cols[pl.ds(col, TOKENS, stride=ROWS), :])
        xt[col] = column
        normed = norm_over(column, 0).astype(BF16)
        gate_t[col] = sigmoid(dot(wt_mix[0], normed, NN))
        return carry

    lax.fori_loop(0, ROWS, column_gate, 0, unroll=2)
    v_aug[...] = jnp.ones(v_aug.shape, BF16)
    q_diag[...] = jnp.zeros(q_diag.shape, BF16)

    for quarter in range(PARTS):
        wait_bytes(lr_recv.at[quarter], lr_recv_sem.at[quarter])
        both = lr_recv[quarter].astype(F32)
        left = both[:, :ROWS].reshape(TOKENS, TOKENS).astype(BF16)
        right = both[:, ROWS:].reshape(TOKENS, TOKENS).astype(BF16)
        total = dot(right, left, NT)
        c_stage[quarter] = jnp.concatenate(
            [
                total[:, :128].reshape(DAP, ROWS, 128),
                total[:, 128:].reshape(DAP, ROWS, 128),
            ],
            axis=1,
        ).astype(BF16)
        exchange(
            c_stage.at[quarter],
            c_recv.at[quarter],
            c_send.at[quarter],
            c_recv_sem.at[quarter],
        )
        if quarter == 1:
            relay(w_expand, 2)
        if quarter == 2:
            relay(w_reduce, 3)

    wait_bytes(w_expand.at[0], relay_recv.at[2])
    for part in range(8):
        wt_expand[part * C : (part + 1) * C] = transposed(
            w_expand[part // 4, :, :, (part % 4) * C : (part % 4 + 1) * C].reshape(C, C)
        )
    wait_bytes(w_reduce.at[0], relay_recv.at[3])
    blocks = [(half, index) for index in range(dp_count) for half in range(2)]
    for part in range(FF // C):
        own = blocks[part * len(blocks) * C // FF : (part + 1) * len(blocks) * C // FF]
        wt_reduce[:, part * C : (part + 1) * C] = transposed(
            jnp.concatenate([w_reduce[half, index] for half, index in own], axis=0)
        )

    means = []
    squares = []
    zero = jnp.zeros((16, 128), F32)
    for quarter in range(PARTS):
        wait_bytes(c_recv.at[quarter], c_recv_sem.at[quarter])

        def c_sum(step, total):
            for inner in range(4):
                block = step * 4 + inner
                value = c_recv[quarter, block].astype(F32)
                start = pl.multiple_of((quarter * PART + block) * ROWS, ROWS)
                c_values[0, pl.ds(start, ROWS), :] = value[:ROWS]
                c_values[1, pl.ds(start, ROWS), :] = value[ROWS:]
                total = total + value
            return total

        mean = lax.fori_loop(0, PART // 4, c_sum, zero) * (1.0 / PART)

        def c_square(step, total):
            for inner in range(4):
                apart = c_recv[quarter, step * 4 + inner].astype(F32) - mean
                total = total + apart * apart
            return total

        means.append(mean)
        squares.append(lax.fori_loop(0, PART // 4, c_square, zero))
    mean = sum(means) * (1.0 / PARTS)
    variance = sum(
        square + (own - mean) * (own - mean) * PART for square, own in zip(squares, means)
    ) * (1.0 / C)
    scale = lax.rsqrt(variance + EPS)
    c_mean[...] = jnp.concatenate([mean[:ROWS], mean[ROWS:]], axis=1)
    c_scale[...] = jnp.concatenate([scale[:ROWS], scale[ROWS:]], axis=1)

    def column_first(col, carry):
        values = jnp.concatenate(
            [
                c_values[0, pl.ds(col, C, stride=ROWS), :],
                c_values[1, pl.ds(col, C, stride=ROWS), :],
            ],
            axis=1,
        )
        normed = ((values - c_mean[pl.ds(col, 1), :]) * c_scale[pl.ds(col, 1), :]).astype(BF16)
        first = xt[col] + gate_t[col] * dot(wt_mix[1], normed, NN)
        first_t[col] = first
        first_norm = norm_over(first, 0).astype(BF16)
        first_norm_t[col] = first_norm
        bias = dot(wt_mix[7, 0:16], first_norm, NN)[:8]
        slot = col // GROUP
        inner = col - slot * GROUP
        bias_rows[slot, 0, pl.ds(inner, 8, stride=GROUP), :] = bias[:, :128]
        bias_rows[slot, 1, pl.ds(inner, 8, stride=GROUP), :] = bias[:, 128:]
        return carry

    for half in range(2):
        lax.fori_loop(half * GROUP, (half + 1) * GROUP, column_first, 0, unroll=4)
        for lanes in range(2):
            bias_stage[half, :, lanes * 128 : (lanes + 1) * 128] = bias_rows[
                half, lanes, 0 : HEADS * GROUP
            ].astype(BF16)
        for target in same_core:
            pltpu.make_async_remote_copy(
                src_ref=bias_stage.at[half],
                dst_ref=bias_recv.at[half, core, my_chip],
                send_sem=bias_send.at[half],
                recv_sem=bias_recv_sem.at[half],
                device_id={"dap": target},
                device_id_type=MESH,
            ).start()
        pltpu.make_async_copy(
            bias_stage.at[half], bias_recv.at[half, core, my_chip], bias_recv_sem.at[half]
        ).start()
        pending.append((bias_recv.at[half, 0, pl.ds(0, DAP // 2 - 1)], bias_send.at[half]))

    def relay_bias(half):
        wait_bytes(bias_recv.at[half, 0], bias_recv_sem.at[half])
        pltpu.make_async_remote_copy(
            src_ref=bias_recv.at[half, core],
            dst_ref=bias_recv.at[half, core],
            send_sem=bias_relay_send.at[half],
            recv_sem=bias_relay_recv.at[half],
            device_id={"dap": sibling},
            device_id_type=MESH,
        ).start()
        pending.append((bias_recv.at[half, 0], bias_relay_send.at[half]))

    q_scale = LOG2E / HEAD**0.5

    def column_project(col, carry):
        first_norm = first_norm_t[col]
        query = (dot(wt_mix[2], first_norm, NN) * q_scale).astype(BF16)
        value = dot(wt_mix[4], first_norm, NN).astype(BF16)
        og_t[col] = sigmoid(dot(wt_mix[5], first_norm, NN))
        k_cols[col] = transposed(dot(wt_mix[3], first_norm, NN))
        for head in range(HEADS):
            rows = slice(head * HEAD, (head + 1) * HEAD)
            q_diag[col, rows, head * TOKENS : (head + 1) * TOKENS] = query[rows]
            v_aug[col, head, 0:HEAD, :] = value[rows]
        return carry

    lax.fori_loop(0, ROWS, column_project, 0, unroll=2)

    relay_bias(0)
    def column_scores(col, carry):
        for head in range(HEADS):
            lanes = slice(head * TOKENS, (head + 1) * TOKENS)
            scores_ref[col, :, lanes] = dot(k_cols[col], q_diag[col, :, lanes], NN)
        return carry

    lax.fori_loop(0, ROWS, column_scores, 0)
    relay_bias(1)
    for half in range(2):
        wait_bytes(bias_recv.at[half, 0], bias_relay_recv.at[half])
    masked = jnp.where(
        lax.broadcasted_iota(jnp.int32, (TOKENS, TOKENS), 0) < length, 0.0, -1e9
    )
    for pair in range(HEADS // 2):
        tiles = []
        for half in range(2):
            by_core = bias_recv[half].astype(F32)[:, :, pair * 8 : pair * 8 + 8]
            by_chip = [by_core[own, chip] for chip in range(DAP // 2) for own in range(2)]
            tiles.append(jnp.stack(by_chip, axis=0))
        low = lax.broadcasted_iota(jnp.int32, (DAP, 8, TOKENS), 1) < GROUP
        swapped = [pltpu.roll(tile, GROUP, 1) for tile in tiles]
        heads = (
            jnp.where(low, tiles[0], swapped[1]),
            jnp.where(low, swapped[0], tiles[1]),
        )
        for inner in range(2):
            turned = jnp.transpose(heads[inner].reshape(TOKENS, TOKENS))
            head = pair * 2 + inner
            bias_t[:, head * TOKENS : (head + 1) * TOKENS] = turned * LOG2E + masked

    def column_attend(two, carry):
        cols = [two * 2, two * 2 + 1]
        seconds = []
        for col in cols:
            scores = [
                scores_ref[col, :, head * TOKENS : (head + 1) * TOKENS]
                + bias_t[:, head * TOKENS : (head + 1) * TOKENS]
                for head in range(HEADS)
            ]
            softs = [
                jnp.exp2(score - jnp.max(score, axis=0, keepdims=True)).astype(BF16)
                for score in scores
            ]
            sums = [dot(v_aug[col, head], softs[head], NN) for head in range(HEADS)]
            attended = jnp.concatenate(
                [total[0:HEAD] * (1.0 / total[HEAD : HEAD + 1]) for total in sums], axis=0
            )
            gated = (attended * og_t[col]).astype(BF16)
            seconds.append(first_t[col] + dot(wt_mix[6], gated, NN))
        norms = [norm_over(second, 0).astype(BF16) for second in seconds]
        hiddens = [dot(wt_expand[0:FF], norm, NN) for norm in norms]
        ups = [dot(wt_expand[FF : 2 * FF], norm, NN) for norm in norms]
        activated = [
            (hidden * sigmoid(hidden) * up).astype(BF16) for hidden, up in zip(hiddens, ups)
        ]
        results = [
            jnp.transpose(second + dot(wt_reduce[...], act, NN)).reshape(DAP, ROWS, C)
            for second, act in zip(seconds, activated)
        ]
        out_stage[two] = jnp.concatenate(results, axis=1).astype(BF16)
        exchange(out_stage.at[two], out_recv.at[two], out_send.at[two], out_recv_sem.at[two])
        pending.pop()
        return carry

    lax.fori_loop(0, ROWS // 2, column_attend, 0, unroll=2)

    for two in range(ROWS // 2):
        wait_bytes(out_recv.at[two], out_recv_sem.at[two])
        out_rows[:, two * 16 : (two + 1) * 16] = out_recv[two].astype(F32)
    flat_rows = out_rows.reshape(TOKENS * ROWS, C)

    def store_row(row, carry):
        out_ref[0, row] = flat_rows[pl.ds(row, TOKENS, stride=ROWS), :].astype(BF16)
        return carry

    lax.fori_loop(0, ROWS, store_row, 0, unroll=4)

    for two in range(ROWS // 2):
        wait_bytes(out_stage.at[two, pl.ds(0, DAP - 1)], out_send.at[two])
    for ref, sem in pending:
        wait_bytes(ref, sem)


def fused(dp_count, pair_repr, lengths, *weights):
    slice_rows = C // dp_count
    vmem = pl.BlockSpec(memory_space=pltpu.VMEM)
    anywhere = pl.BlockSpec(memory_space=pltpu.HBM)
    scratch = [
        pltpu.VMEM((1, ROWS, TOKENS, C), BF16),
        pltpu.VMEM((HEADS, slice_rows), BF16),
        pltpu.VMEM((C, C), F32),
        pltpu.VMEM((slice_rows, 4 * C), BF16),
        pltpu.VMEM((PARTS, slice_rows, C), BF16),
        pltpu.VMEM((2, slice_rows, FF), BF16),
        pltpu.VMEM((PARTS, dp_count, slice_rows, C), BF16),
        pltpu.VMEM((2, dp_count, slice_rows, FF), BF16),
        pltpu.VMEM((2, dp_count, slice_rows, FF), BF16),
        pltpu.VMEM((2, dp_count, FF // dp_count // 2, C), BF16),
        pltpu.VMEM((PARTS, C, C), BF16),
        pltpu.VMEM((8, C, C), BF16),
        pltpu.VMEM((2 * FF, C), BF16),
        pltpu.VMEM((C, FF), BF16),
        pltpu.VMEM((DAP, 64, C), BF16),
        pltpu.VMEM((DAP, 64, C), BF16),
        pltpu.VMEM((ROWS, TOKENS, C), BF16),
        pltpu.VMEM((2, 2, PART * ROWS, 128), F32),
        pltpu.VMEM((PARTS, DAP, 16, TOKENS), BF16),
        pltpu.VMEM((PARTS, DAP, 16, TOKENS), BF16),
        pltpu.VMEM((PARTS, DAP, 16, 128), BF16),
        pltpu.VMEM((PARTS, DAP, 16, 128), BF16),
        pltpu.VMEM((2, C * ROWS, 128), F32),
        pltpu.VMEM((ROWS, TOKENS), F32),
        pltpu.VMEM((ROWS, TOKENS), F32),
        pltpu.VMEM((TOKENS * ROWS, C), F32),
        pltpu.VMEM((ROWS, C, TOKENS), F32),
        pltpu.VMEM((ROWS, C, TOKENS), F32),
        pltpu.VMEM((ROWS, C, TOKENS), F32),
        pltpu.VMEM((ROWS, C, TOKENS), BF16),
        pltpu.VMEM((2, 2, 8 * GROUP, 128), F32),
        pltpu.VMEM((2, HEADS * GROUP, TOKENS), BF16),
        pltpu.VMEM((2, 2, DAP // 2, HEADS * GROUP, TOKENS), BF16),
        pltpu.VMEM((TOKENS, HEADS * TOKENS), F32),
        pltpu.VMEM((ROWS, C, HEADS * TOKENS), BF16),
        pltpu.VMEM((ROWS, TOKENS, C), BF16),
        pltpu.VMEM((ROWS, HEADS, 48, TOKENS), BF16),
        pltpu.VMEM((ROWS, C, TOKENS), F32),
        pltpu.VMEM((ROWS, TOKENS, HEADS * TOKENS), F32),
        pltpu.VMEM((ROWS // 2, DAP, 16, C), BF16),
        pltpu.VMEM((ROWS // 2, DAP, 16, C), BF16),
        pltpu.VMEM((DAP, 64, C), F32),
        pltpu.SemaphoreType.DMA((4 + PARTS,)),
        pltpu.SemaphoreType.DMA((4 + PARTS,)),
        pltpu.SemaphoreType.DMA((4,)),
        pltpu.SemaphoreType.DMA((4,)),
        pltpu.SemaphoreType.DMA((2,)),
        pltpu.SemaphoreType.DMA((PARTS,)),
        pltpu.SemaphoreType.DMA((PARTS,)),
        pltpu.SemaphoreType.DMA((PARTS,)),
        pltpu.SemaphoreType.DMA((PARTS,)),
        pltpu.SemaphoreType.DMA((2,)),
        pltpu.SemaphoreType.DMA((2,)),
        pltpu.SemaphoreType.DMA((2,)),
        pltpu.SemaphoreType.DMA((2,)),
        pltpu.SemaphoreType.DMA((ROWS // 2,)),
        pltpu.SemaphoreType.DMA((ROWS // 2,)),
        pltpu.SemaphoreType.DMA((8,)),
        pltpu.SemaphoreType.REGULAR,
    ]
    return pl.pallas_call(
        functools.partial(body, dp_count),
        out_shape=jax.ShapeDtypeStruct((1, ROWS, TOKENS, C), BF16),
        in_specs=[pl.BlockSpec(memory_space=pltpu.SMEM)] + [anywhere] * 9,
        out_specs=vmem,
        scratch_shapes=scratch,
        compiler_params=pltpu.CompilerParams(
            collective_id=0, has_side_effects=True, vmem_limit_bytes=VMEM_LIMIT
        ),
    )(lengths, pair_repr, *weights[:4], jnp.transpose(weights[4]), *weights[5:])


def solution(mesh):
    dp_count = mesh.shape["dp"]
    placed = (P("dp", "dap", None, None), P("dp")) + (P("dp", None),) * 8
    return jax.shard_map(
        functools.partial(fused, dp_count),
        mesh=mesh,
        in_specs=placed,
        out_specs=P("dp", "dap", None, None),
        check_vma=False,
    )
```

time: 70.7 us -> 63.3 us (0.90)
  Pallas kernels: 68 us -> 60.6 us
    pallas_call x1, Pallas kernels: 68 us -> 60.6 us  [fused(): pl.pallas_call(functools.partial(body, dp_count), out_shape=jax.ShapeDtyp...]
where the time goes in v3:
time: 63.3 us; the launch traced here: 63.2 us
  Pallas kernels  60.6 us (96%)
  local copies, waits for them, and re-layouts  1.87 us (3%)
  between operations  0.66 us (1%)
    pallas_call x1, Pallas kernels, fused(): pl.pallas_call(functools.partial(body, dp_count), out_shape=jax.ShapeDtyp...  60.6 us
    unnamed x1, local copies, waits for them, and re-layouts  1.87 us

profile of v3, /device:TPU:1, one launch (start us, length us, event | category | flops | bytes accessed | tf_op | source)
XLA Modules:
  0.0 63.2 jit_solution(3650426318928871253)
XLA Ops:
  0.7 60.6 %shard_map.100 = bf16[1,8,256,128]{3,2,1,0:T(8,128)(2,1)} custom-call(s32[1]{0:T(128)S(6)} %copy.12.length_ref, bf16[1,8,256,128]{3,2,1,0:T(8,128)(2,1)} %x_hbm.1, bf16[16,512]{1,0:T(8,128)(2,1)} %tri_project_ref.1, bf16[16,128]{1,0:T(8,128)(2,1)} %tri_gate_ref.1, bf16[16,128]{1,0:T(8,128)(2,1)} %tri_output_ref.1, bf16[16,512]{1,0:T(8,128)(2,1)} %attn_project_ref.1, ...), custom_call_target="tpu_custom_call" | custom-call | tf_op jit(solution)/shard_map/pallas_call | solution.py:637
  61.3 1.9 %copy.13 = bf16[1,8,256,128]{3,2,1,0:T(8,128)(2,1)} copy(bf16[1,8,256,128]{3,2,1,0:T(8,128)(2,1)} %shard_map.100) | data formatting | bytes 1048576

commit v4 on v3

--- a/solution.py
+++ b/solution.py
@@ -70,7 +70,7 @@
     attn_output_ref,
     expand_ref,
     reduce_ref,
-    out_ref,
+    out_recv,
     x_ref,
     bias_in,
     bias_square,
@@ -110,9 +110,8 @@
     v_aug,
     og_t,
     scores_ref,
+    second_t,
     out_stage,
-    out_recv,
-    out_rows,
     w_send,
     w_recv,
     relay_send,
@@ -516,10 +515,9 @@
             head = pair * 2 + inner
             bias_t[:, head * TOKENS : (head + 1) * TOKENS] = turned * LOG2E + masked
 
-    def column_attend(two, carry):
-        cols = [two * 2, two * 2 + 1]
+    def attend(two):
         seconds = []
-        for col in cols:
+        for col in (two * 2, two * 2 + 1):
             scores = [
                 scores_ref[col, :, head * TOKENS : (head + 1) * TOKENS]
                 + bias_t[:, head * TOKENS : (head + 1) * TOKENS]
@@ -535,6 +533,9 @@
             )
             gated = (attended * og_t[col]).astype(BF16)
             seconds.append(first_t[col] + dot(wt_mix[6], gated, NN))
+        return seconds
+
+    def transition(two, seconds):
         norms = [norm_over(second, 0).astype(BF16) for second in seconds]
         hiddens = [dot(wt_expand[0:FF], norm, NN) for norm in norms]
         ups = [dot(wt_expand[FF : 2 * FF], norm, NN) for norm in norms]
@@ -546,22 +547,27 @@
             for second, act in zip(seconds, activated)
         ]
         out_stage[two] = jnp.concatenate(results, axis=1).astype(BF16)
+
+    def send_out(two):
         exchange(out_stage.at[two], out_recv.at[two], out_send.at[two], out_recv_sem.at[two])
         pending.pop()
+
+    second_t[0], second_t[1] = attend(0)
+
+    def column_attend(two, carry):
+        before = [second_t[0], second_t[1]]
+        transition(two - 1, before)
+        after = attend(two)
+        send_out(two - 1)
+        second_t[0], second_t[1] = after
         return carry
 
-    lax.fori_loop(0, ROWS // 2, column_attend, 0, unroll=2)
+    lax.fori_loop(1, ROWS // 2, column_attend, 0)
+    transition(ROWS // 2 - 1, [second_t[0], second_t[1]])
+    send_out(ROWS // 2 - 1)
 
     for two in range(ROWS // 2):
         wait_bytes(out_recv.at[two], out_recv_sem.at[two])
-        out_rows[:, two * 16 : (two + 1) * 16] = out_recv[two].astype(F32)
-    flat_rows = out_rows.reshape(TOKENS * ROWS, C)
-
-    def store_row(row, carry):
-        out_ref[0, row] = flat_rows[pl.ds(row, TOKENS, stride=ROWS), :].astype(BF16)
-        return carry
-
-    lax.fori_loop(0, ROWS, store_row, 0, unroll=4)
 
     for two in range(ROWS // 2):
         wait_bytes(out_stage.at[two, pl.ds(0, DAP - 1)], out_send.at[two])
@@ -569,9 +575,28 @@
         wait_bytes(ref, sem)
 
 
+def to_rows(blocks_ref, out_ref, blocks, wide, rows, load_sems, store_sems):
+    loads = [
+        pltpu.make_async_copy(blocks_ref.at[two], blocks.at[two], load_sems.at[two])
+        for two in range(ROWS // 2)
+    ]
+    for load in loads:
+        load.start()
+    for two, load in enumerate(loads):
+        load.wait()
+        wide[:, two * 16 : (two + 1) * 16] = blocks[two].astype(F32)
+    flat = wide.reshape(TOKENS * ROWS, C)
+    stores = []
+    for row in range(ROWS):
+        rows[row] = flat[pl.ds(row, TOKENS, stride=ROWS), :].astype(BF16)
+        stores.append(pltpu.make_async_copy(rows.at[row], out_ref.at[0, row], store_sems.at[row]))
+        stores[-1].start()
+    for store in stores:
+        store.wait()
+
+
 def fused(dp_count, pair_repr, lengths, *weights):
     slice_rows = C // dp_count
-    vmem = pl.BlockSpec(memory_space=pltpu.VMEM)
     anywhere = pl.BlockSpec(memory_space=pltpu.HBM)
     scratch = [
         pltpu.VMEM((1, ROWS, TOKENS, C), BF16),
@@ -613,9 +638,8 @@
         pltpu.VMEM((ROWS, HEADS, 48, TOKENS), BF16),
         pltpu.VMEM((ROWS, C, TOKENS), F32),
         pltpu.VMEM((ROWS, TOKENS, HEADS * TOKENS), F32),
+        pltpu.VMEM((2, C, TOKENS), F32),
         pltpu.VMEM((ROWS // 2, DAP, 16, C), BF16),
-        pltpu.VMEM((ROWS // 2, DAP, 16, C), BF16),
-        pltpu.VMEM((DAP, 64, C), F32),
         pltpu.SemaphoreType.DMA((4 + PARTS,)),
         pltpu.SemaphoreType.DMA((4 + PARTS,)),
         pltpu.SemaphoreType.DMA((4,)),
@@ -634,16 +658,30 @@
         pltpu.SemaphoreType.DMA((8,)),
         pltpu.SemaphoreType.REGULAR,
     ]
-    return pl.pallas_call(
+    blocks = pl.pallas_call(
         functools.partial(body, dp_count),
-        out_shape=jax.ShapeDtypeStruct((1, ROWS, TOKENS, C), BF16),
+        out_shape=jax.ShapeDtypeStruct((ROWS // 2, DAP, 16, C), BF16),
         in_specs=[pl.BlockSpec(memory_space=pltpu.SMEM)] + [anywhere] * 9,
-        out_specs=vmem,
+        out_specs=anywhere,
         scratch_shapes=scratch,
         compiler_params=pltpu.CompilerParams(
             collective_id=0, has_side_effects=True, vmem_limit_bytes=VMEM_LIMIT
         ),
     )(lengths, pair_repr, *weights[:4], jnp.transpose(weights[4]), *weights[5:])
+    return pl.pallas_call(
+        to_rows,
+        out_shape=jax.ShapeDtypeStruct((1, ROWS, TOKENS, C), BF16),
+        in_specs=[anywhere],
+        out_specs=anywhere,
+        scratch_shapes=[
+            pltpu.VMEM((ROWS // 2, DAP, 16, C), BF16),
+            pltpu.VMEM((DAP, 64, C), F32),
+            pltpu.VMEM((ROWS, TOKENS, C), BF16),
+            pltpu.SemaphoreType.DMA((ROWS // 2,)),
+            pltpu.SemaphoreType.DMA((ROWS,)),
+        ],
+        compiler_params=pltpu.CompilerParams(vmem_limit_bytes=VMEM_LIMIT),
+    )(blocks)
 
 
 def solution(mesh):

time: 63.3 us -> 62.5 us (0.987)
  local copies, waits for them, and re-layouts: 1.87 us -> 0 us
  Pallas kernels: 60.6 us -> 61.7 us
    pallas_call x0 -> x1, Pallas kernels: none -> 2.03 us  [fused(): pl.pallas_call(to_rows, out_shape=jax.ShapeDtypeStruct((1, ROWS, TOKENS,...]
    unnamed x1 -> x0, local copies, waits for them, and re-layouts: 1.87 us -> none
    pallas_call x1, Pallas kernels: 60.6 us -> 59.7 us  [fused(): pl.pallas_call(functools.partial(body, dp_count), out_shape=jax.ShapeDtyp...]
where the time goes in v4:
time: 62.5 us; the launch traced here: 62.4 us
  Pallas kernels  61.7 us (99%)
  between operations  0.66 us (1%)
    pallas_call x1, Pallas kernels, fused(): pl.pallas_call(functools.partial(body, dp_count), out_shape=jax.ShapeDtyp...  59.7 us
    pallas_call x1, Pallas kernels, fused(): pl.pallas_call(to_rows, out_shape=jax.ShapeDtypeStruct((1, ROWS, TOKENS,...  2.03 us

profile of v4, /device:TPU:1, one launch (start us, length us, event | category | flops | bytes accessed | tf_op | source)
XLA Modules:
  0.0 62.4 jit_solution(3794739669152102252)
XLA Ops:
  0.7 59.7 %shard_map.100.blocks_ref = bf16[4,32,16,128]{3,2,1,0:T(8,128)(2,1)} custom-call(s32[1]{0:T(128)S(6)} %copy.11.length_ref, bf16[1,8,256,128]{3,2,1,0:T(8,128)(2,1)} %x_hbm.1, bf16[16,512]{1,0:T(8,128)(2,1)} %tri_project_ref.1, bf16[16,128]{1,0:T(8,128)(2,1)} %tri_gate_ref.1, bf16[16,128]{1,0:T(8,128)(2,1)} %tri_output_ref.1, ...), custom_call_target="tpu_custom_call" | custom-call | tf_op jit(solution)/shard_map/pallas_call | solution.py:661
  60.3 2.0 %shard_map.101 = bf16[1,8,256,128]{3,2,1,0:T(8,128)(2,1)} custom-call(bf16[4,32,16,128]{3,2,1,0:T(8,128)(2,1)} %shard_map.100.blocks_ref), custom_call_target="tpu_custom_call" | custom-call | tf_op jit(solution)/shard_map/pallas_call | solution.py:671

commit v5 on v4

--- a/solution.py
+++ b/solution.py
@@ -297,7 +297,7 @@
                 lr_rows[side, 1, pl.ds(row, PART, stride=ROWS), :] = kept[:, 128:]
             return carry
 
-        lax.fori_loop(0, ROWS, project_row, 0, unroll=4)
+        lax.fori_loop(0, ROWS, project_row, 0, unroll=8)
         for lanes in range(2):
             lr_stage[quarter, :, :, lanes * 128 : (lanes + 1) * 128] = jnp.concatenate(
                 [lr_rows[side, lanes].reshape(DAP, ROWS, 128) for side in range(2)], axis=1
@@ -341,7 +341,7 @@
         gate_t[col] = sigmoid(dot(wt_mix[0], normed, NN))
         return carry
 
-    lax.fori_loop(0, ROWS, column_gate, 0, unroll=2)
+    lax.fori_loop(0, ROWS, column_gate, 0, unroll=4)
     v_aug[...] = jnp.ones(v_aug.shape, BF16)
     q_diag[...] = jnp.zeros(q_diag.shape, BF16)
 
@@ -482,7 +482,7 @@
             v_aug[col, head, 0:HEAD, :] = value[rows]
         return carry
 
-    lax.fori_loop(0, ROWS, column_project, 0, unroll=2)
+    lax.fori_loop(0, ROWS, column_project, 0, unroll=4)
 
     relay_bias(0)
     def column_scores(col, carry):
@@ -491,7 +491,7 @@
             scores_ref[col, :, lanes] = dot(k_cols[col], q_diag[col, :, lanes], NN)
         return carry
 
-    lax.fori_loop(0, ROWS, column_scores, 0)
+    lax.fori_loop(0, ROWS, column_scores, 0, unroll=2)
     relay_bias(1)
     for half in range(2):
         wait_bytes(bias_recv.at[half, 0], bias_relay_recv.at[half])
@@ -535,7 +535,7 @@
             seconds.append(first_t[col] + dot(wt_mix[6], gated, NN))
         return seconds
 
-    def transition(two, seconds):
+    def transition(seconds):
         norms = [norm_over(second, 0).astype(BF16) for second in seconds]
         hiddens = [dot(wt_expand[0:FF], norm, NN) for norm in norms]
         ups = [dot(wt_expand[FF : 2 * FF], norm, NN) for norm in norms]
@@ -543,10 +543,10 @@
             (hidden * sigmoid(hidden) * up).astype(BF16) for hidden, up in zip(hiddens, ups)
         ]
         results = [
-            jnp.transpose(second + dot(wt_reduce[...], act, NN)).reshape(DAP, ROWS, C)
+            jnp.transpose(second + dot(wt_reduce[...], act, NN)).reshape(-1, ROWS, C)
             for second, act in zip(seconds, activated)
         ]
-        out_stage[two] = jnp.concatenate(results, axis=1).astype(BF16)
+        return jnp.concatenate(results, axis=1).astype(BF16)
 
     def send_out(two):
         exchange(out_stage.at[two], out_recv.at[two], out_send.at[two], out_recv_sem.at[two])
@@ -556,15 +556,42 @@
 
     def column_attend(two, carry):
         before = [second_t[0], second_t[1]]
-        transition(two - 1, before)
+        out_stage[two - 1] = transition(before)
         after = attend(two)
         send_out(two - 1)
         second_t[0], second_t[1] = after
         return carry
 
     lax.fori_loop(1, ROWS // 2, column_attend, 0)
-    transition(ROWS // 2 - 1, [second_t[0], second_t[1]])
-    send_out(ROWS // 2 - 1)
+    last = ROWS // 2 - 1
+    for half in range(2):
+        owners = DAP // 2
+        lanes = slice(half * 128, (half + 1) * 128)
+        out_stage[last, half * owners : (half + 1) * owners] = transition(
+            [second_t[0, :, lanes], second_t[1, :, lanes]]
+        )
+        targets = [half * owners + (me + step) % owners for step in range(owners)]
+        send_blocks(
+            targets[1:],
+            out_stage.at[last],
+            out_recv.at[last],
+            out_send.at[last],
+            out_recv_sem.at[last],
+        )
+
+        @pl.when(me // owners != half)
+        def _():
+            send_blocks(
+                targets[:1],
+                out_stage.at[last],
+                out_recv.at[last],
+                out_send.at[last],
+                out_recv_sem.at[last],
+            )
+
+    pltpu.make_async_copy(
+        out_stage.at[last, me], out_recv.at[last, me], out_recv_sem.at[last]
+    ).start()
 
     for two in range(ROWS // 2):
         wait_bytes(out_recv.at[two], out_recv_sem.at[two])

time: 62.5 us -> 62 us (level)
  no operation moved by 1% of the time
where the time goes in v5:
time: 62 us; the launch traced here: 61.9 us
  Pallas kernels  61.2 us (99%)
  between operations  0.66 us (1%)
    pallas_call x1, Pallas kernels, fused(): pl.pallas_call(functools.partial(body, dp_count), out_shape=jax.ShapeDtyp...  59.2 us
    pallas_call x1, Pallas kernels, fused(): pl.pallas_call(to_rows, out_shape=jax.ShapeDtypeStruct((1, ROWS, TOKENS,...  2.03 us

profile of v5, /device:TPU:1, one launch (start us, length us, event | category | flops | bytes accessed | tf_op | source)
XLA Modules:
  0.0 61.9 jit_solution(13025415887945207722)
XLA Ops:
  0.7 59.2 %shard_map.100.blocks_ref = bf16[4,32,16,128]{3,2,1,0:T(8,128)(2,1)} custom-call(s32[1]{0:T(128)S(6)} %copy.11.length_ref, bf16[1,8,256,128]{3,2,1,0:T(8,128)(2,1)} %x_hbm.1, bf16[16,512]{1,0:T(8,128)(2,1)} %tri_project_ref.1, bf16[16,128]{1,0:T(8,128)(2,1)} %tri_gate_ref.1, bf16[16,128]{1,0:T(8,128)(2,1)} %tri_output_ref.1, ...), custom_call_target="tpu_custom_call" | custom-call | tf_op jit(solution)/shard_map/pallas_call | solution.py:688
  59.8 2.0 %shard_map.101 = bf16[1,8,256,128]{3,2,1,0:T(8,128)(2,1)} custom-call(bf16[4,32,16,128]{3,2,1,0:T(8,128)(2,1)} %shard_map.100.blocks_ref), custom_call_target="tpu_custom_call" | custom-call | tf_op jit(solution)/shard_map/pallas_call | solution.py:698

commit v6 on v5

--- a/solution.py
+++ b/solution.py
@@ -111,6 +111,7 @@
     og_t,
     scores_ref,
     second_t,
+    unit,
     out_stage,
     w_send,
     w_recv,
@@ -485,13 +486,18 @@
     lax.fori_loop(0, ROWS, column_project, 0, unroll=4)
 
     relay_bias(0)
+    unit[...] = (
+        lax.broadcasted_iota(jnp.int32, (TOKENS, TOKENS), 0)
+        == lax.broadcasted_iota(jnp.int32, (TOKENS, TOKENS), 1)
+    ).astype(F32).astype(BF16)
+
     def column_scores(col, carry):
         for head in range(HEADS):
             lanes = slice(head * TOKENS, (head + 1) * TOKENS)
             scores_ref[col, :, lanes] = dot(k_cols[col], q_diag[col, :, lanes], NN)
         return carry
 
-    lax.fori_loop(0, ROWS, column_scores, 0, unroll=2)
+    lax.fori_loop(0, ROWS, column_scores, 0, unroll=4)
     relay_bias(1)
     for half in range(2):
         wait_bytes(bias_recv.at[half, 0], bias_relay_recv.at[half])
@@ -511,7 +517,7 @@
             jnp.where(low, swapped[0], tiles[1]),
         )
         for inner in range(2):
-            turned = jnp.transpose(heads[inner].reshape(TOKENS, TOKENS))
+            turned = dot(unit[...], heads[inner].reshape(TOKENS, TOKENS).astype(BF16), NT)
             head = pair * 2 + inner
             bias_t[:, head * TOKENS : (head + 1) * TOKENS] = turned * LOG2E + masked
 
@@ -562,7 +568,7 @@
         second_t[0], second_t[1] = after
         return carry
 
-    lax.fori_loop(1, ROWS // 2, column_attend, 0)
+    lax.fori_loop(1, ROWS // 2, column_attend, 0, unroll=3)
     last = ROWS // 2 - 1
     for half in range(2):
         owners = DAP // 2
@@ -666,6 +672,7 @@
         pltpu.VMEM((ROWS, C, TOKENS), F32),
         pltpu.VMEM((ROWS, TOKENS, HEADS * TOKENS), F32),
         pltpu.VMEM((2, C, TOKENS), F32),
+        pltpu.VMEM((TOKENS, TOKENS), BF16),
         pltpu.VMEM((ROWS // 2, DAP, 16, C), BF16),
         pltpu.SemaphoreType.DMA((4 + PARTS,)),
         pltpu.SemaphoreType.DMA((4 + PARTS,)),

time: 62 us -> 60.9 us (0.982)
  Pallas kernels: 61.2 us -> 60.1 us
    pallas_call x1, Pallas kernels: 59.2 us -> 58.1 us  [fused(): pl.pallas_call(functools.partial(body, dp_count), out_shape=jax.ShapeDtyp...]
where the time goes in v6:
time: 60.9 us; the launch traced here: 60.8 us
  Pallas kernels  60.1 us (99%)
  between operations  0.66 us (1%)
    pallas_call x1, Pallas kernels, fused(): pl.pallas_call(functools.partial(body, dp_count), out_shape=jax.ShapeDtyp...  58.1 us
    pallas_call x1, Pallas kernels, fused(): pl.pallas_call(to_rows, out_shape=jax.ShapeDtypeStruct((1, ROWS, TOKENS,...  2.03 us

profile of v6, /device:TPU:1, one launch (start us, length us, event | category | flops | bytes accessed | tf_op | source)
XLA Modules:
  0.0 60.8 jit_solution(16893350681849929150)
XLA Ops:
  0.7 58.1 %shard_map.100.blocks_ref = bf16[4,32,16,128]{3,2,1,0:T(8,128)(2,1)} custom-call(s32[1]{0:T(128)S(6)} %copy.11.length_ref, bf16[1,8,256,128]{3,2,1,0:T(8,128)(2,1)} %x_hbm.1, bf16[16,512]{1,0:T(8,128)(2,1)} %tri_project_ref.1, bf16[16,128]{1,0:T(8,128)(2,1)} %tri_gate_ref.1, bf16[16,128]{1,0:T(8,128)(2,1)} %tri_output_ref.1, ...), custom_call_target="tpu_custom_call" | custom-call | tf_op jit(solution)/shard_map/pallas_call | solution.py:695
  58.8 2.0 %shard_map.101 = bf16[1,8,256,128]{3,2,1,0:T(8,128)(2,1)} custom-call(bf16[4,32,16,128]{3,2,1,0:T(8,128)(2,1)} %shard_map.100.blocks_ref), custom_call_target="tpu_custom_call" | custom-call | tf_op jit(solution)/shard_map/pallas_call | solution.py:705
